TPU v7x, 256 devices: a whole 4x4x8 slice. The times are simulated.
256 devices in a mesh: seq: 16 (over y, z_hi), tp: 4 (over x), dp: 4 (over z_lo, core).
Axes of the slice: x: 4, y: 4, z: 8 (z_hi: 4, z_lo: 2; z = z_hi * 2 + z_lo), core: 2. Of those that a mesh axis runs over, the one named last changes fastest.
Arguments:
- seq_input: bfloat16 [4, 16384, 8192], P('tp', 'seq', 'dp'), may hold values from -4 to 4
- seq_b: bfloat16 [4, 16384, 1024], P('tp', 'seq', 'dp'), may hold values from -0.5 to 0.5
- seq_c: bfloat16 [4, 16384, 1024], P('tp', 'seq', 'dp'), may hold values from -0.5 to 0.5
- seq_decay: float32 [4, 128, 16384], P('tp', 'dp', 'seq'), may hold values from -1 to 0, as said below
- row_prompt: int32 [256], P(('seq', 'dp')), may hold values from 0 to 3
- cache_slot: int32 [256], P(('seq', 'dp')), may hold values from 0 to 3, as said below
- step_input: bfloat16 [8, 256, 8192], P(None, ('seq', 'dp'), 'tp'), may hold values from -8 to 8
- step_b: bfloat16 [8, 256, 1024], P(None, ('seq', 'dp'), 'tp'), may hold values from -0.5 to 0.5
- step_c: bfloat16 [8, 256, 1024], P(None, ('seq', 'dp'), 'tp'), may hold values from -0.5 to 0.5
- step_decay: float32 [8, 256, 128], P(None, ('seq', 'dp'), 'tp'), may hold values from 0.5 to 1
Outputs:
- seq_output: bfloat16 [4, 16384, 8192], P('tp', 'seq', 'dp')
- step_output: bfloat16 [8, 256, 8192], P(None, ('seq', 'dp'), 'tp')
- state_cache: bfloat16 [256, 128, 64, 128], P(('seq', 'dp'), 'tp')
Inputs may be any that keep to these rules, and one draw needn't show every extreme that they name: `seq_decay`: every entry is negative. `cache_slot`: each aligned block of 4 rows holds each of 0 to 3 once.
All inputs are finite; a program needn't handle non-finite values.
Results may differ from a plain program's by a relative error of at most 0.0055.
Values sent between devices are 32-bit elements; how exact they have to be, the bound alone decides.
A program may use at most 128 MiB of HBM per device.

v0:
```python
import jax
import jax.numpy as jnp
from jax import lax
from jax.sharding import PartitionSpec as P

P_SIZE = 64
N = 128
Q = 256
STEPS = 8


HIGH = lax.Precision.HIGHEST


def prefix(part, axis, combine, identity):
    place = lax.axis_index(axis)
    gathered = jax.tree.map(lambda a: lax.all_gather(a, axis), part)
    state = jax.tree.map(lambda a, e: jnp.zeros_like(a) + jnp.asarray(e, a.dtype), part, identity)

    def one(hop, state):
        return combine(
            state, jax.tree.map(lambda a: lax.dynamic_index_in_dim(a, hop, 0, False), gathered)
        )

    return lax.fori_loop(0, place, one, state)


def from_root(block, axis, owner):
    block = jnp.where(lax.axis_index(axis) == owner, block, jnp.zeros_like(block))
    return lax.psum(block, axis)


def chain_combine(earlier, later):
    return (earlier[0] + later[0], jnp.exp(later[0])[:, None, None] * earlier[1] + later[1])


def per_device(
    seq_input,
    seq_b,
    seq_c,
    seq_decay,
    row_prompt,
    cache_slot,
    step_input,
    step_b,
    step_c,
    step_decay,
):
    length = seq_input.shape[1]
    groups = seq_b.shape[2] // N
    heads = seq_decay.shape[1]
    per_group = heads // groups
    count = length // Q
    inputs = seq_input.reshape(count, Q, groups, per_group, P_SIZE)
    b_blocks = seq_b.reshape(count, Q, groups, N)
    c_blocks = seq_c.reshape(count, Q, groups, N)
    cumulative = jnp.cumsum(seq_decay.reshape(heads, count, Q), axis=-1)
    cumulative = cumulative.transpose(1, 0, 2).reshape(count, groups, per_group, Q)
    lower = jnp.tril(jnp.ones((Q, Q), dtype=bool))

    def inner_block(fragments):
        x_block, b_block, c_block, cum_block = fragments
        scores = jnp.einsum("ign,jgn->gij", c_block, b_block, preferred_element_type=jnp.float32)
        gaps = cum_block[:, :, :, None] - cum_block[:, :, None, :]
        weights = (scores[:, None] * jnp.exp(jnp.where(lower, gaps, -jnp.inf))).astype(jnp.bfloat16)
        return jnp.einsum("ghij,jghp->ighp", weights, x_block, preferred_element_type=jnp.float32)

    inner = lax.map(inner_block, (inputs, b_blocks, c_blocks, cumulative))
    last = cumulative[..., -1:]
    scaled = (jnp.exp(last - cumulative).transpose(0, 3, 1, 2)[..., None] * inputs).astype(
        jnp.bfloat16
    )
    terms = jnp.einsum("cjghp,cjgn->cghpn", scaled, b_blocks, preferred_element_type=jnp.float32)
    totals = last[..., 0]

    def local_step(state, fragments):
        total, term = fragments
        return (jnp.exp(total)[..., None, None] * state + term, state)

    own_state, before = lax.scan(
        local_step, jnp.zeros(terms.shape[1:], jnp.float32), (totals, terms)
    )
    lead = jnp.cumsum(totals, axis=0) - totals
    flat_decay = jnp.sum(totals, axis=0).reshape(heads)
    flat_state = own_state.reshape(heads, P_SIZE, N)
    prior = prefix(
        (flat_decay, flat_state),
        "seq",
        chain_combine,
        (jnp.zeros_like(flat_decay), jnp.zeros_like(flat_state)),
    )
    entering = prior[1]
    closing = chain_combine(prior, (flat_decay, flat_state))[1]
    final = from_root(closing, "seq", lax.axis_size("seq") - 1)
    entering_groups = entering.reshape(groups, per_group, P_SIZE, N)
    starts = (jnp.exp(lead)[..., None, None] * entering_groups + before).astype(jnp.bfloat16)
    carried = jnp.einsum("cign,cghpn->cighp", c_blocks, starts, preferred_element_type=jnp.float32)
    carried = carried * jnp.exp(cumulative).transpose(0, 3, 1, 2)[..., None]
    seq_output = (inner + carried).astype(jnp.bfloat16).reshape(1, length, heads * P_SIZE)
    heads_all = heads * lax.axis_size("dp")
    parts = lax.axis_size("tp")
    spread = lax.all_gather(final.reshape(1, heads, P_SIZE, N), "dp", axis=1, tiled=True)
    owned = lax.all_to_all(
        spread.reshape(1, parts, heads_all // parts, P_SIZE, N),
        "tp",
        split_axis=1,
        concat_axis=0,
        tiled=True,
    )
    owned = owned.reshape(parts, heads_all // parts, P_SIZE, N)
    rows = row_prompt.shape[0]
    dec_heads = step_decay.shape[2]
    dec_groups = step_b.shape[2] // N
    dec_per = dec_heads // dec_groups
    state = jnp.take(owned, row_prompt, axis=0).reshape(rows, dec_groups, dec_per, P_SIZE, N)
    answers = []
    for step in range(STEPS):
        x_heads = step_input[step].reshape(rows, dec_groups, dec_per, P_SIZE).astype(jnp.float32)
        b_group = step_b[step].reshape(rows, dec_groups, N).astype(jnp.float32)
        c_group = step_c[step].reshape(rows, dec_groups, N).astype(jnp.float32)
        keep = step_decay[step].reshape(rows, dec_groups, dec_per)
        state = keep[..., None, None] * state + x_heads[..., None] * b_group[:, :, None, None, :]
        answers.append(
            jnp.einsum("rghpn,rgn->rghp", state, c_group, precision=HIGH).reshape(
                rows, dec_heads * P_SIZE
            )
        )
    step_output = jnp.stack(answers).astype(jnp.bfloat16)
    finished = state.astype(jnp.bfloat16).reshape(rows, dec_heads, P_SIZE, N)
    state_cache = jnp.zeros_like(finished).at[cache_slot].set(finished)
    return (seq_output, step_output, state_cache)


def solution(mesh):
    return jax.shard_map(
        per_device,
        mesh=mesh,
        in_specs=(
            P("tp", "seq", "dp"),
            P("tp", "seq", "dp"),
            P("tp", "seq", "dp"),
            P("tp", "dp", "seq"),
            P(("seq", "dp")),
            P(("seq", "dp")),
            P(None, ("seq", "dp"), "tp"),
            P(None, ("seq", "dp"), "tp"),
            P(None, ("seq", "dp"), "tp"),
            P(None, ("seq", "dp"), "tp"),
        ),
        out_specs=(
            P("tp", "seq", "dp"),
            P(None, ("seq", "dp"), "tp"),
            P(("seq", "dp"), "tp", None, None),
        ),
        check_vma=False,
    )
```

profile of v0, /device:TPU:7, one launch (start us, length us, event | category | flops | bytes accessed | tf_op | source)
XLA Modules:
  0.0 656.8 jit_solution(17234570276492840507)
XLA Ops:
  7.2 1.0 reshape.284
  8.3 2.3 reduce-window.6
  11.3 6.4 copy.35
  17.8 7.9 %reshape.281 = bf16[4,256,2,16,64]{1,0,4,3,2:T(4,128)(2,1)} reshape(bf16[1,1024,2048]{1,2,0:T(8,128)(2,1)} %copy.35) | data formatting | bytes 8388608 | tf_op jit(solution)/shard_map/reshape | solution.py:54
  25.8 4.3 multiply_convert_fusion.4
  30.1 3.3 fusion.15
  33.4 10.1 %while.38 = (s32[]{:T(128)}, f32[2,16,64,128]{3,2,1,0:T(8,128)S(1)}, f32[4,2,16,64,128]{4,3,2,1,0:T(8,128)}, f32[4,2,16]{2,1,0:T(2,128)S(1)}, f32[4,2,16,64,128]{4,3,2,1,0:T(8,128)}, /*index=5*/s32[]{:T(128)}, s32[]{:T(128)}) while((s32[]{:T(128)}, f32[2,16,64,128]{3,2,1,0:T(8,128)S(1)}, f32[4,2,16,64,128]{4,3,2,1,0:T(8,128)}, ...), condition=%wide.region_7.8_spmd.clone, body=%wide.region_6.7_spmd.clone.sunk | while | flops 1048579 | bytes 5243872 | solution.py:80
  33.4 1.1 bitcast_dynamic-update-slice_fusion.5
  34.5 1.4 bitcast_add_fusion.6
  35.9 1.1 bitcast_dynamic-update-slice_fusion.5
  37.0 1.4 bitcast_add_fusion.6
  38.4 1.1 bitcast_dynamic-update-slice_fusion.5
  39.5 1.4 bitcast_add_fusion.6
  40.9 1.1 bitcast_dynamic-update-slice_fusion.5
  42.1 1.4 bitcast_add_fusion.6
  43.5 1.0 copy-done
  44.7 39.7 %all-gather = f32[16,1,32]{2,1,0:T(1,128)S(1)} all-gather(f32[1,1,32]{2,1,0:T(1,128)S(1)} %reshape.334), channel_id=1, replica_groups=mesh['seq'=16,'tp'=4,'dp'=4] {'seq'}, dimensions={0}, use_global_device_ids=true | all-gather | bytes 2176 | tf_op jit(solution)/shard_map/all_gather | solution.py:17
  84.4 153.5 %all-gather.4.cloned.1.call-done = f32[16,32,64,128]{3,2,1,0:T(8,128)} async-done(((f32[1,32,64,128]{3,2,1,0:T(8,128)}), f32[16,32,64,128]{3,2,1,0:T(8,128)}) %all-gather.4.cloned.1.call-update) | async-done | bytes 16777232 | tf_op jit(solution)/shard_map/all_gather | solution.py:17
  238.1 1.2 copy-done.1
  239.3 1.1 fusion.63
  240.5 191.3 %all-reduce.2.cloned.1.call-done = f32[1,32,64,128]{3,2,0,1:T(8,128)} async-done(((f32[1,32,64,128]{3,2,0,1:T(8,128)}), f32[1,32,64,128]{3,2,0,1:T(8,128)}) %all-reduce.2.cloned.1.call-update) | async-done | bytes 1048592 | tf_op jit(solution)/shard_map/psum | solution.py:30
  432.1 0.7 reshape.294
  437.2 5.1 copy.38
  457.6 1.2 compare_select_fusion
  458.9 32.0 %all-gather.6.cloned.1.call-done = f32[1,128,64,128]{3,2,0,1:T(8,128)} async-done(((f32[1,32,64,128]{3,2,0,1:T(8,128)}), f32[1,128,64,128]{3,2,0,1:T(8,128)}) %all-gather.6.cloned.1.call-update) | async-done | bytes 4194320 | tf_op jit(solution)/shard_map/all_gather | solution.py:102
  490.8 5.1 all-to-all-start
  495.9 19.0 %while.37 = (s32[]{:T(128)}, f32[4,256,2,16,64]{1,4,3,2,0:T(8,128)}, bf16[4,256,2,16,64]{1,4,3,2,0:T(8,128)(2,1)}, bf16[4,256,2,128]{3,2,1,0:T(2,128)(2,1)S(1)},...) while((s32[]{:T(128)}, f32[4,256,2,16,64]{1,4,3,2,0:T(8,128)}, ...), condition=%wide.region_3.4_spmd.clone, body=%wide.region_2.3_spmd.clone.sunk | while | flops 310444032 | bytes 5243989 | solution.py:68
  496.4 4.3 bitcast_dynamic-update-slice_fusion.4
  501.1 4.3 bitcast_dynamic-update-slice_fusion.4
  505.9 4.3 bitcast_dynamic-update-slice_fusion.4
  510.6 4.3 bitcast_dynamic-update-slice_fusion.4
  514.9 8.0 %fusion.14 = bf16[4,256,2,16,64]{1,4,3,2,0:T(8,128)(2,1)} fusion(f32[4,256,2,16,64]{1,4,3,2,0:T(8,128)} %get-tuple-element.112, f32[4,256,2,16]{1,3,2,0:T(8,128)S(1)} %get-tuple-element.220, f32[4,2,16,64,128]{4,3,2,1,0:T(8,128)} %get-tuple-element.115, f32[2,16,64,128]{3,2,1,0:T(8,128)S(1)} %bitcast.157, f32[4,2,16]{2,1,0:T(2,128)S(1)} %fusion.62, ...), kind=kOutput, calls=%fused_computation.29 | convolution fusion | flops 546308096 | bytes 18481664 | tf_op jit(solution)/shard_map/cign,cghpn->cighp/dot_general | solution.py:97
  522.9 13.0 %copy.70 = bf16[4,256,2,16,64]{4,3,2,1,0:T(8,128)(2,1)} copy(bf16[4,256,2,16,64]{1,4,3,2,0:T(8,128)(2,1)} %fusion.14) | data formatting | bytes 8388608
  535.9 12.3 %reshape.355 = bf16[1,1024,2048]{2,1,0:T(8,128)(2,1)} reshape(bf16[4,256,2,16,64]{4,3,2,1,0:T(8,128)(2,1)} %copy.70) | data formatting | bytes 8388608
  548.3 5.0 gather_fusion
  553.3 7.7 %fusion.21 = f32[4,2,1,16,64]{4,2,3,1,0:T(1,128)S(1)} fusion(bf16[4,2,128,1,1]{2,3,4,1,0:T(2,128)(2,1)S(1)} %copy-done.44, f32[4,2,16,64,128]{4,3,2,1,0:T(8,128)} %bitcast.158, f32[4,2,128]{2,1,0:T(2,128)S(1)} %reshape.295, f32[4,2,16,64]{3,2,1,0:T(8,128)S(1)} %copy-done.6, f32[4,2,16]{2,1,0:T(2,128)S(1)} %copy-done.15, f32[4,2,128]{2,1,0:T(2,128)S(1)} %reshape.293, ...), kind=kOutput, calls=%fused_computation.46 | convolution fusion | flops 19922944 | bytes 4303876 | tf_op jit(solution)/shard_map/rghpn,rgn->rghp/dot_general | solution.py:124
  561.1 6.9 %fusion.25 = f32[4,2,1,16,64]{4,2,3,1,0:T(1,128)S(1)} fusion(bf16[4,2,128,1,1]{2,3,4,1,0:T(2,128)(2,1)S(1)} %copy-done.43, f32[4,2,16,64,128]{4,3,2,1,0:T(8,128)} %bitcast.159, f32[4,2,128]{2,1,0:T(2,128)S(1)} %reshape.293, f32[4,2,16,64]{3,2,1,0:T(8,128)S(1)} %reshape.292, f32[4,2,16]{2,1,0:T(2,128)S(1)} %copy-done.14, pred[4]{0:T(512)(128)(4,1)S(1)} %compare_and_fusion), kind=kOutput, calls=%fused_computation.50 | convolution fusion | flops 16777216 | bytes 4266500 | tf_op jit(solution)/shard_map/rghpn,rgn->rghp/dot_general | solution.py:124
  568.2 7.2 %multiply_add_fusion.4 = f32[4,2,16,64,128]{4,3,2,1,0:T(8,128)S(1)} fusion(f32[4,2,16,64,128]{4,3,2,1,0:T(8,128)} %bitcast.160, f32[4,2,128]{2,1,0:T(2,128)S(1)} %reshape.297, f32[4,2,16,64]{3,2,1,0:T(8,128)S(1)} %copy-done.7, f32[4,2,16]{2,1,0:T(2,128)S(1)} %copy-done.16, f32[4,2,128]{2,1,0:T(2,128)S(1)} %reshape.295, f32[4,2,16,64]{3,2,1,0:T(8,128)S(1)} %copy-done.6, ...), kind=kLoop, calls=%fused_computation.42 | loop fusion | flops 10485760 | bytes 8500740 | tf_op jit(solution)/shard_map/add | solution.py:122
  575.5 2.0 copy-done.2
  577.6 5.0 fusion.71
  582.7 6.9 %fusion.22 = f32[4,2,1,16,64]{4,2,3,1,0:T(1,128)S(1)} fusion(bf16[4,2,128,1,1]{2,3,4,1,0:T(2,128)(2,1)S(1)} %copy-done.19, f32[4,2,16,64,128]{4,3,2,1,0:T(8,128)} %copy-done.2, f32[4,2,128]{2,1,0:T(2,128)S(1)} %copy-done.13, f32[4,2,16,64]{3,2,1,0:T(8,128)S(1)} %reshape.298, f32[4,2,16]{2,1,0:T(2,128)S(1)} %copy-done.17), kind=kOutput, calls=%fused_computation.47 | convolution fusion | flops 15728640 | bytes 4266496 | tf_op jit(solution)/shard_map/rghpn,rgn->rghp/dot_general | solution.py:124
  589.7 7.7 %fusion.68 = f32[4,2,1,16,64]{4,2,3,1,0:T(1,128)S(1)} fusion(bf16[4,2,128,1,1]{2,3,4,1,0:T(2,128)(2,1)S(1)} %copy-done.40, f32[4,2,16,64,128]{4,3,2,1,0:T(8,128)} %copy-done.2, f32[4,2,128]{2,1,0:T(2,128)S(1)} %copy-done.22, f32[4,2,16,64]{3,2,1,0:T(8,128)S(1)} %copy-done.9, f32[4,2,16]{2,1,0:T(2,128)S(1)} %copy-done.35, f32[4,2,128]{2,1,0:T(2,128)S(1)} %copy-done.13, ...), kind=kOutput, calls=%fused_computation.138 | convolution fusion | flops 18874368 | bytes 4303872 | tf_op jit(solution)/shard_map/rghpn,rgn->rghp/dot_general | solution.py:124
  597.6 8.9 %fusion.23 = f32[4,2,1,16,64]{4,2,3,1,0:T(1,128)S(1)} fusion(bf16[4,2,128,1,1]{2,3,4,1,0:T(2,128)(2,1)S(1)} %copy-done.41, f32[4,2,128]{2,1,0:T(2,128)S(1)} %copy-done.23, f32[4,2,16,64]{3,2,1,0:T(8,128)S(1)} %copy-done.10, f32[4,2,16]{2,1,0:T(2,128)S(1)} %copy-done.36, f32[4,2,16,64,128]{4,3,2,1,0:T(8,128)} %copy-done.2, f32[4,2,128]{2,1,0:T(2,128)S(1)} %copy-done.22, ...), kind=kOutput, calls=%fused_computation.48 | convolution fusion | flops 22020096 | bytes 4341248 | tf_op jit(solution)/shard_map/rghpn,rgn->rghp/dot_general | solution.py:124
  606.7 10.7 %fusion.24 = f32[4,2,1,16,64]{4,2,3,1,0:T(1,128)S(1)} fusion(bf16[4,2,128,1,1]{2,3,4,1,0:T(2,128)(2,1)S(1)} %copy-done.42, f32[4,2,128]{2,1,0:T(2,128)S(1)} %copy-done.24, f32[4,2,16,64]{3,2,1,0:T(8,128)S(1)} %copy-done.11, f32[4,2,16]{2,1,0:T(2,128)S(1)} %copy-done.37, f32[4,2,128]{2,1,0:T(2,128)S(1)} %copy-done.23, f32[4,2,16,64]{3,2,1,0:T(8,128)S(1)} %copy-done.10, ...), kind=kOutput, calls=%fused_computation.49 | convolution fusion | flops 25165824 | bytes 4378624 | tf_op jit(solution)/shard_map/rghpn,rgn->rghp/dot_general | solution.py:124
  617.7 12.0 %fusion.17 = f32[4,2,1,16,64]{4,2,3,1,0:T(1,128)S(1)} fusion(bf16[4,2,128,1,1]{2,3,4,1,0:T(2,128)(2,1)S(1)} %copy-done.39, f32[4,2,128]{2,1,0:T(2,128)S(1)} %copy-done.25, f32[4,2,16,64]{3,2,1,0:T(8,128)S(1)} %copy-done.12, f32[4,2,16]{2,1,0:T(2,128)S(1)} %copy-done.38, f32[4,2,128]{2,1,0:T(2,128)S(1)} %copy-done.24, f32[4,2,16,64]{3,2,1,0:T(8,128)S(1)} %copy-done.11, ...), kind=kOutput, calls=%fused_computation.34 | convolution fusion | flops 28311552 | bytes 4416000 | tf_op jit(solution)/shard_map/rghpn,rgn->rghp/dot_general | solution.py:124
  630.1 15.0 %add_convert_fusion = bf16[4,32,64,128]{3,2,1,0:T(8,128)(2,1)} fusion(f32[4,32,64,128]{3,2,1,0:T(8,128)} %gather_fusion, f32[4,32,128]{2,1,0:T(8,128)S(1)} %bitcast.174, f32[4,32,64]{2,1,0:T(8,128)S(1)} %reshape.315, f32[4,32,128]{2,1,0:T(8,128)S(1)} %bitcast.172, f32[4,32,64]{2,1,0:T(8,128)S(1)} %reshape.314, f32[4,32,128]{2,1,0:T(8,128)S(1)} %bitcast.170, ...), kind=kLoop, calls=%fused_computation.33 | loop fusion | flops 27262976 | bytes 7081988 | tf_op jit(solution)/shard_map/convert_element_type | solution.py:129
  645.6 3.3 scatter_fusion
  648.9 1.3 copy-done.3
  (215 shorter events, 24.8 us)
Async XLA Ops:
  7.2 230.7 %all-gather.4.cloned.1.call-start = ((), (), s32[]{:S(2)}) async-start(), calls=%async_computation.1 | async-start | bytes 17825792 | tf_op jit(solution)/shard_map/all_gather | solution.py:17
  17.8 7.9 %copy-start.4 = (bf16[1,1024,256]{2,1,0:T(8,128)(2,1)S(1)}, bf16[1,1024,256]{2,1,0:T(8,128)(2,1)}, u32[]{:S(2)}) copy-start(bf16[1,1024,256]{2,1,0:T(8,128)(2,1)} %param.17) | copy-start | bytes 1572868
  44.5 387.3 %all-reduce.2.cloned.1.call-start = ((), (), s32[]{:S(2)}) async-start(), calls=%async_computation.2 | async-start | bytes 2097152 | tf_op jit(solution)/shard_map/psum | solution.py:30
  238.1 193.8 %copy-start.8 = (bf16[8,4,2048]{2,1,0:T(4,128)(2,1)S(1)}, bf16[8,4,2048]{2,1,0:T(4,128)(2,1)}, u32[]{:S(2)}) copy-start(bf16[8,4,2048]{2,1,0:T(4,128)(2,1)} %param.22) | copy-start | bytes 393220
  240.4 250.4 %all-gather.6.cloned.1.call-start = ((), (), s32[]{:S(2)}) async-start(), calls=%async_computation.3 | async-start | bytes 5242880 | tf_op jit(solution)/shard_map/all_gather | solution.py:102
  437.2 5.1 copy-start.20
  437.2 7.1 %copy-start.21 = (bf16[8,4,256]{2,1,0:T(4,128)(2,1)S(1)}, bf16[8,4,256]{2,1,0:T(4,128)(2,1)}, u32[]{:S(2)}) copy-start(bf16[8,4,256]{2,1,0:T(4,128)(2,1)} %param.23) | copy-start | bytes 49156
  437.2 7.1 %copy-start.26 = (bf16[8,4,256]{2,1,0:T(4,128)(2,1)S(1)}, bf16[8,4,256]{2,1,0:T(4,128)(2,1)}, u32[]{:S(2)}) copy-start(bf16[8,4,256]{2,1,0:T(4,128)(2,1)} %param.24) | copy-start | bytes 49156
  437.2 18.9 %copy-start.5 = (bf16[1,1024,256]{2,1,0:T(8,128)(2,1)S(1)}, bf16[1,1024,256]{2,1,0:T(8,128)(2,1)}, u32[]{:S(2)}) copy-start(bf16[1,1024,256]{2,1,0:T(8,128)(2,1)} %param.18) | copy-start | bytes 1572868
  490.8 57.4 %all-to-all-start = ((f32[1,4,32,64,128]{4,3,2,0,1:T(8,128)}), f32[1,4,32,64,128]{4,3,2,0,1:T(8,128)}, u32[]{:S(2)}, u32[]{:S(2)}) async-start(f32[1,4,32,64,128]{4,3,2,0,1:T(8,128)} %bitcast.163), calls=%async_computation | async-start | bytes 8388608 | tf_op jit(solution)/shard_map/all_to_all | solution.py:103
  548.3 5.0 copy-start.6
  548.3 5.0 copy-start.14
  548.3 5.0 copy-start.15
  548.3 5.0 copy-start.44
  553.3 7.8 %copy-start.43 = (bf16[4,2,128,1,1]{2,3,4,1,0:T(2,128)(2,1)S(1)}, bf16[4,2,128,1,1]{2,3,4,1,0:T(2,128)(2,1)}, u32[]{:S(2)}) copy-start(bf16[4,2,128,1,1]{2,3,4,1,0:T(2,128)(2,1)} %reshape.357) | copy-start | bytes 6148
  561.0 7.2 %copy-start.7 = (f32[4,2,16,64]{3,2,1,0:T(8,128)S(1)}, f32[4,2,16,64]{3,2,1,0:T(8,128)}, u32[]{:S(2)}) copy-start(f32[4,2,16,64]{3,2,1,0:T(8,128)} %reshape.296) | copy-start | bytes 98308
  561.0 7.2 %copy-start.16 = (f32[4,2,16]{2,1,0:T(2,128)S(1)}, f32[4,2,16]{2,1,0:T(2,128)}, u32[]{:S(2)}) copy-start(f32[4,2,16]{2,1,0:T(2,128)} %mul.417) | copy-start | bytes 1540
  568.2 9.3 %copy-start.18 = (bf16[4,2,128,1,1]{2,3,4,1,0:T(2,128)(2,1)S(1)}, bf16[4,2,128,1,1]{2,3,4,1,0:T(2,128)(2,1)}, u32[]{:S(2)}) copy-start(bf16[4,2,128,1,1]{2,3,4,1,0:T(2,128)(2,1)} %reshape.361) | copy-start | bytes 6148
  575.5 2.0 copy-start.2
  577.5 5.1 copy-start.13
  577.5 5.1 copy-start.17
  577.5 5.2 copy-start.19
  577.5 12.2 %copy-start.9 = (f32[4,2,16,64]{3,2,1,0:T(8,128)S(1)}, f32[4,2,16,64]{3,2,1,0:T(8,128)}, u32[]{:S(2)}) copy-start(f32[4,2,16,64]{3,2,1,0:T(8,128)} %reshape.300) | copy-start | bytes 98308
  577.5 12.2 %copy-start.22 = (f32[4,2,128]{2,1,0:T(2,128)S(1)}, f32[4,2,128]{2,1,0:T(2,128)}, u32[]{:S(2)}) copy-start(f32[4,2,128]{2,1,0:T(2,128)} %reshape.301) | copy-start | bytes 12292
  577.5 12.2 %copy-start.35 = (f32[4,2,16]{2,1,0:T(2,128)S(1)}, f32[4,2,16]{2,1,0:T(2,128)}, u32[]{:S(2)}) copy-start(f32[4,2,16]{2,1,0:T(2,128)} %mul.429) | copy-start | bytes 1540
  577.5 12.2 %copy-start.40 = (bf16[4,2,128,1,1]{2,3,4,1,0:T(2,128)(2,1)S(1)}, bf16[4,2,128,1,1]{2,3,4,1,0:T(2,128)(2,1)}, u32[]{:S(2)}) copy-start(bf16[4,2,128,1,1]{2,3,4,1,0:T(2,128)(2,1)} %reshape.365) | copy-start | bytes 6148
  589.5 8.0 %copy-start.10 = (f32[4,2,16,64]{3,2,1,0:T(8,128)S(1)}, f32[4,2,16,64]{3,2,1,0:T(8,128)}, u32[]{:S(2)}) copy-start(f32[4,2,16,64]{3,2,1,0:T(8,128)} %reshape.302) | copy-start | bytes 98308
  589.6 8.0 %copy-start.23 = (f32[4,2,128]{2,1,0:T(2,128)S(1)}, f32[4,2,128]{2,1,0:T(2,128)}, u32[]{:S(2)}) copy-start(f32[4,2,128]{2,1,0:T(2,128)} %reshape.303) | copy-start | bytes 12292
  589.6 8.0 %copy-start.36 = (f32[4,2,16]{2,1,0:T(2,128)S(1)}, f32[4,2,16]{2,1,0:T(2,128)}, u32[]{:S(2)}) copy-start(f32[4,2,16]{2,1,0:T(2,128)} %mul.435) | copy-start | bytes 1540
  589.6 8.0 %copy-start.41 = (bf16[4,2,128,1,1]{2,3,4,1,0:T(2,128)(2,1)S(1)}, bf16[4,2,128,1,1]{2,3,4,1,0:T(2,128)(2,1)}, u32[]{:S(2)}) copy-start(bf16[4,2,128,1,1]{2,3,4,1,0:T(2,128)(2,1)} %reshape.367) | copy-start | bytes 6148
  597.6 9.1 %copy-start.11 = (f32[4,2,16,64]{3,2,1,0:T(8,128)S(1)}, f32[4,2,16,64]{3,2,1,0:T(8,128)}, u32[]{:S(2)}) copy-start(f32[4,2,16,64]{3,2,1,0:T(8,128)} %reshape.304) | copy-start | bytes 98308
  597.6 9.1 %copy-start.24 = (f32[4,2,128]{2,1,0:T(2,128)S(1)}, f32[4,2,128]{2,1,0:T(2,128)}, u32[]{:S(2)}) copy-start(f32[4,2,128]{2,1,0:T(2,128)} %reshape.305) | copy-start | bytes 12292
  597.6 9.1 %copy-start.37 = (f32[4,2,16]{2,1,0:T(2,128)S(1)}, f32[4,2,16]{2,1,0:T(2,128)}, u32[]{:S(2)}) copy-start(f32[4,2,16]{2,1,0:T(2,128)} %mul.441) | copy-start | bytes 1540
  597.6 9.1 %copy-start.42 = (bf16[4,2,128,1,1]{2,3,4,1,0:T(2,128)(2,1)S(1)}, bf16[4,2,128,1,1]{2,3,4,1,0:T(2,128)(2,1)}, u32[]{:S(2)}) copy-start(bf16[4,2,128,1,1]{2,3,4,1,0:T(2,128)(2,1)} %reshape.369) | copy-start | bytes 6148
  606.7 10.9 %copy-start.12 = (f32[4,2,16,64]{3,2,1,0:T(8,128)S(1)}, f32[4,2,16,64]{3,2,1,0:T(8,128)}, u32[]{:S(2)}) copy-start(f32[4,2,16,64]{3,2,1,0:T(8,128)} %reshape.306) | copy-start | bytes 98308
  606.7 10.9 %copy-start.25 = (f32[4,2,128]{2,1,0:T(2,128)S(1)}, f32[4,2,128]{2,1,0:T(2,128)}, u32[]{:S(2)}) copy-start(f32[4,2,128]{2,1,0:T(2,128)} %reshape.307) | copy-start | bytes 12292
  606.7 10.9 %copy-start.38 = (f32[4,2,16]{2,1,0:T(2,128)S(1)}, f32[4,2,16]{2,1,0:T(2,128)}, u32[]{:S(2)}) copy-start(f32[4,2,16]{2,1,0:T(2,128)} %mul.447) | copy-start | bytes 1540
  606.7 10.9 %copy-start.39 = (bf16[4,2,128,1,1]{2,3,4,1,0:T(2,128)(2,1)S(1)}, bf16[4,2,128,1,1]{2,3,4,1,0:T(2,128)(2,1)}, u32[]{:S(2)}) copy-start(bf16[4,2,128,1,1]{2,3,4,1,0:T(2,128)(2,1)} %reshape.371) | copy-start | bytes 6148
  617.6 12.4 %copy-start.27 = (f32[4,32]{1,0:T(4,128)S(1)}, f32[4,32]{1,0:T(4,128)}, u32[]{:S(2)}) copy-start(f32[4,32]{1,0:T(4,128)} %get-tuple-element.221) | copy-start | bytes 1540
  617.6 12.4 %copy-start.28 = (f32[4,32]{1,0:T(4,128)S(1)}, f32[4,32]{1,0:T(4,128)}, u32[]{:S(2)}) copy-start(f32[4,32]{1,0:T(4,128)} %get-tuple-element.222) | copy-start | bytes 1540
  617.6 12.4 %copy-start.29 = (f32[4,32]{1,0:T(4,128)S(1)}, f32[4,32]{1,0:T(4,128)}, u32[]{:S(2)}) copy-start(f32[4,32]{1,0:T(4,128)} %get-tuple-element.223) | copy-start | bytes 1540
  617.6 12.4 %copy-start.30 = (f32[4,32]{1,0:T(4,128)S(1)}, f32[4,32]{1,0:T(4,128)}, u32[]{:S(2)}) copy-start(f32[4,32]{1,0:T(4,128)} %get-tuple-element.224) | copy-start | bytes 1540
  617.6 12.4 %copy-start.31 = (f32[4,32]{1,0:T(4,128)S(1)}, f32[4,32]{1,0:T(4,128)}, u32[]{:S(2)}) copy-start(f32[4,32]{1,0:T(4,128)} %get-tuple-element.225) | copy-start | bytes 1540
  617.6 12.4 %copy-start.32 = (f32[4,32]{1,0:T(4,128)S(1)}, f32[4,32]{1,0:T(4,128)}, u32[]{:S(2)}) copy-start(f32[4,32]{1,0:T(4,128)} %get-tuple-element.226) | copy-start | bytes 1540
  617.7 12.4 %copy-start.33 = (f32[4,32]{1,0:T(4,128)S(1)}, f32[4,32]{1,0:T(4,128)}, u32[]{:S(2)}) copy-start(f32[4,32]{1,0:T(4,128)} %get-tuple-element.227) | copy-start | bytes 1540
  617.7 12.4 %copy-start.34 = (f32[4,32]{1,0:T(4,128)S(1)}, f32[4,32]{1,0:T(4,128)}, u32[]{:S(2)}) copy-start(f32[4,32]{1,0:T(4,128)} %get-tuple-element.228) | copy-start | bytes 1540
  629.9 15.7 %copy-start.45 = (bf16[8,4,2048]{2,1,0:T(4,128)(2,1)}, bf16[8,4,2048]{2,1,0:T(4,128)(2,1)S(1)}, u32[]{:S(2)}) copy-start(bf16[8,4,2048]{2,1,0:T(4,128)(2,1)S(1)} %constant_dynamic-update-slice_fusion) | copy-start | bytes 393220
  630.1 15.5 %copy-start.46 = (s32[4]{0:T(128)S(1)}, s32[4]{0:T(128)}, u32[]{:S(2)}) copy-start(s32[4]{0:T(128)} %compare_select_fusion) | copy-start | bytes 52
  (3 other events, 3.5 us)
Sparse Core Ops, SparseCore 0:
  44.6 193.2 all-gather.3
  241.1 190.6 all-reduce.1
  433.8 57.0 all-gather.5
where the time goes:
time: 660 us; the launch traced here: 657 us
  waiting for transfers between devices  377 us (57%)
  matrix products  95 us (14%)
  local copies, waits for them, and re-layouts  81.9 us (12%)
  other arithmetic  43.2 us (7%)
  blocking collectives  39.7 us (6%)
  between operations  14.7 us (2%)
    psum x1, waiting for transfers between devices, from_root(): return lax.psum(block, axis)  191 us
    all_gather x1, waiting for transfers between devices, prefix(): gathered = jax.tree.map(lambda a: lax.all_gather(a, axis), part)  154 us
    dot_general x8, matrix products, per_device(): jnp.einsum('rghpn,rgn->rghp', state, c_group, precision=HIGH)  65.7 us
    unnamed x106, local copies, waits for them, and re-layouts  42.6 us
    all_gather x1, blocking collectives, prefix(): gathered = jax.tree.map(lambda a: lax.all_gather(a, axis), part)  39.7 us
    all_gather x1, waiting for transfers between devices, per_device(): lax.all_gather(final.reshape(1, heads, P_SIZE, N), 'dp', axis=1, tiled=True)  32 us
    dot_general x4, matrix products, inner_block(): jnp.einsum('ghij,jghp->ighp', weights, x_block, preferred_element_type=jn...  17.1 us
    convert_element_type x1, other arithmetic, per_device(): finished = state.astype(jnp.bfloat16).reshape(rows, dec_heads, P_SIZE, N)  15 us
  transfers between devices with their start and end apart: 4, of which 3 were waited for; matrix products, arithmetic and copies ran while one was open for 12% of the time, Pallas kernels for 0%

commit v1 on v0

v1 whole, which is shorter than its diff:
```python
import functools
import math

import jax
import jax.numpy as jnp
import numpy as np
from jax import lax
from jax.experimental import pallas as pl
from jax.experimental.pallas import tpu as pltpu
from jax.sharding import PartitionSpec as P

MESH = pl.DeviceIdType.MESH
P_SIZE = 64
N = 128
B = 128
STEPS = 8
LOG2E = math.log2(math.e)
HIGH = lax.Precision.HIGHEST
F32 = jnp.float32
BF16 = jnp.bfloat16
CH = 4
MIB = 2**20


def dot(a, b, dims=((1,), (0,)), precision=None):
    return lax.dot_general(
        a, b, (dims, ((), ())), preferred_element_type=F32, precision=precision
    )


def spread_matrix(heads):
    row = np.arange(2 * heads)[:, None] % heads
    col = np.arange(heads * P_SIZE)[None, :] // P_SIZE
    return jnp.asarray((row == col).astype(np.float32), BF16)


def split_spread(v, spread):
    half = v.shape[1] // 2
    hi = v.astype(BF16)
    low = (v - hi.astype(F32)).astype(BF16)
    lane = lax.broadcasted_iota(jnp.int32, v.shape, 1)
    return dot(jnp.where(lane < half, hi, low), spread)


def block_sums(dec):
    dec2 = jnp.concatenate([dec, dec], axis=0) * LOG2E
    row = lax.broadcasted_iota(jnp.int32, (B, B), 0)
    col = lax.broadcasted_iota(jnp.int32, (B, B), 1)
    upper = (row <= col).astype(F32)
    cum = dot(dec2, upper, precision=HIGH)
    return cum, cum.T


def prep_kernel(x_ref, b_ref, c_ref, d_ref, spread_ref, y_ref, s_ref, state, total):
    k = pl.program_id(0)
    heads = d_ref.shape[0]
    groups = b_ref.shape[1] // N
    per = heads // groups
    wide = per * P_SIZE

    @pl.when(k == 0)
    def _():
        state[...] = jnp.zeros_like(state)
        total[...] = jnp.zeros_like(total)

    cum, cum_t = block_sums(d_ref[...])
    last = cum_t[B - 1 : B, :]
    spread = spread_ref[...]
    row = lax.broadcasted_iota(jnp.int32, (B, B), 0)
    col = lax.broadcasted_iota(jnp.int32, (B, B), 1)
    lane = lax.broadcasted_iota(jnp.int32, (B, 2 * P_SIZE), 1)
    for g in range(groups):
        lanes = pl.ds(g * wide, wide)
        spread_g = spread[:, g * wide : (g + 1) * wide]
        b = b_ref[:, g * N : (g + 1) * N]
        c = c_ref[:, g * N : (g + 1) * N]
        x = x_ref[:, lanes]
        before = state[:, lanes]
        grown = split_spread(jnp.exp2(cum_t), spread_g)
        carried = dot(c, before.astype(BF16)) * grown
        left = split_spread(jnp.exp2(last - cum_t), spread_g)
        scaled = (x.astype(F32) * left).astype(BF16)
        term = dot(b.T, scaled)
        keep = split_spread(jnp.broadcast_to(jnp.exp2(last), (8, 2 * heads)), spread_g)
        state[:, lanes] = before * keep[0:1, :] + term
        scores = jnp.where(row >= col, dot(c, b, ((1,), (1,))), 0.0)
        for pair in range(per // 2):
            weights = []
            for h in (g * per + 2 * pair, g * per + 2 * pair + 1):
                gap = jnp.minimum(cum_t[:, h : h + 1] - cum[h : h + 1, :], 0.0)
                weights.append((scores * jnp.exp2(gap)).astype(BF16))
            xp = x[:, pair * 2 * P_SIZE : (pair + 1) * 2 * P_SIZE]
            zero = jnp.zeros_like(xp)
            both = jnp.concatenate(
                [jnp.where(lane < P_SIZE, xp, zero), jnp.where(lane < P_SIZE, zero, xp)], axis=0
            )
            inner = dot(jnp.concatenate(weights, axis=1), both)
            at = pl.ds(g * wide + pair * 2 * P_SIZE, 2 * P_SIZE)
            y_ref[:, at] = (
                inner + carried[:, pair * 2 * P_SIZE : (pair + 1) * 2 * P_SIZE]
            ).astype(y_ref.dtype)
    total[...] += jnp.broadcast_to(last, total.shape)

    @pl.when(k == pl.num_programs(0) - 1)
    def _():
        keep = split_spread(jnp.exp2(total[...]), spread)
        for pair in range(heads // 2):
            at = pl.ds(pair * 2 * P_SIZE, 2 * P_SIZE)
            s_ref[pair, 0:N, :] = state[:, at]
            s_ref[pair, N : N + 8, :] = keep[:, pair * 2 * P_SIZE : (pair + 1) * 2 * P_SIZE]


def close_kernel(y_ref, c_ref, d_ref, e_ref, spread_ref, out_ref, enter, total):
    k = pl.program_id(0)
    groups = c_ref.shape[1] // N
    wide = y_ref.shape[1] // groups

    @pl.when(k == 0)
    def _():
        total[...] = jnp.zeros_like(total)
        for pair in range(e_ref.shape[0]):
            enter[:, pair * 2 * P_SIZE : (pair + 1) * 2 * P_SIZE] = e_ref[pair].astype(BF16)

    _, cum_t = block_sums(d_ref[...])
    grown = jnp.exp2(cum_t + total[0:1, :])
    for g in range(groups):
        lanes = pl.ds(g * wide, wide)
        carried = dot(c_ref[:, g * N : (g + 1) * N], enter[:, lanes])
        factor = split_spread(grown, spread_ref[:, g * wide : (g + 1) * wide])
        out_ref[:, lanes] = (y_ref[:, lanes].astype(F32) + carried * factor).astype(BF16)
    total[...] += jnp.broadcast_to(cum_t[B - 1 : B, :], total.shape)


def scan_kernel(
    sizes,
    s_ref,
    e_ref,
    g_ref,
    got,
    tops,
    staged,
    turned,
    z_send,
    z_recv,
    y_send,
    y_recv,
    e_send,
    e_recv,
    swap_send,
    swap_recv,
    fz_send,
    fz_recv,
    fl_send,
    fl_recv,
    fy_send,
    fy_recv,
    fc_send,
    fc_recv,
):
    nz, ny = sizes
    s, t, d = lax.axis_index("seq"), lax.axis_index("tp"), lax.axis_index("dp")
    y, z = s // nz, s % nz
    zl, core = d // 2, d % 2
    away = t != d

    def z_dev(i):
        return (y * nz + (z + i) % nz, t, d)

    def y_dev(i):
        return (((y + i) % ny) * nz + z, t, d)

    swap_dev = (s, d, t)
    zl_dev = (s, t, (1 - zl) * 2 + core)
    core_dev = (s, t, zl * 2 + 1 - core)

    barrier = pltpu.get_barrier_semaphore()
    others = [z_dev(i) for i in range(1, nz)] + [y_dev(i) for i in range(1, ny)]
    others += [zl_dev, core_dev]
    for dev in others:
        pl.semaphore_signal(barrier, inc=1, device_id=dev, device_id_type=MESH)

    @pl.when(away)
    def _():
        pl.semaphore_signal(barrier, inc=1, device_id=swap_dev, device_id_type=MESH)

    pl.semaphore_wait(barrier, jnp.where(away, len(others) + 1, len(others)))

    def copy(src, dst, send, recv, dev):
        return pltpu.make_async_remote_copy(
            src_ref=src, dst_ref=dst, send_sem=send, recv_sem=recv, device_id=dev,
            device_id_type=MESH,
        )

    def z_copy(c, i):
        return copy(
            s_ref.at[CH * ((z + i) % nz) + c], got.at[z, c], z_send.at[c, i - 1],
            z_recv.at[c, i - 1], z_dev(i),
        )

    def y_copy(c, i):
        return copy(
            tops.at[y, c], tops.at[y, c], y_send.at[c, i - 1], y_recv.at[c, i - 1], y_dev(i)
        )

    def e_copy(c, i):
        return copy(
            staged.at[(z + i) % nz, c], e_ref.at[CH * z + c], e_send.at[c, i - 1],
            e_recv.at[c, i - 1], z_dev(i),
        )

    def swap_copy(c):
        return copy(
            turned.at[c, pl.ds(32 * y, 32)], g_ref.at[c, y, t % 2, t // 2, z], swap_send.at[c],
            swap_recv.at[c], swap_dev,
        )

    def fz_copy(c, i):
        ref = g_ref.at[c, y, core, zl, z]
        return copy(ref, ref, fz_send.at[c, i - 1], fz_recv.at[c, i - 1], z_dev(i))

    def fl_copy(c):
        ref = g_ref.at[c, y, core, zl]
        return copy(ref, ref, fl_send.at[c], fl_recv.at[c], zl_dev)

    def fy_copy(c, i):
        ref = g_ref.at[c, y, core]
        return copy(ref, ref, fy_send.at[c, i - 1], fy_recv.at[c, i - 1], y_dev(i))

    def fc_copy(c, i):
        ref = g_ref.at[c, (y + ny - i) % ny, core]
        return copy(ref, ref, fc_send.at[c, i], fc_recv.at[c, i], core_dev)

    for c in range(CH):
        for i in range(1, nz):
            z_copy(c, i).start()
    for c in range(CH):
        got[z, c] = s_ref[CH * z + c]

    def stage_a(c):
        for i in range(1, nz):
            z_copy(c, i).wait_recv()
        top = got[0, c, 0:N]
        keep = got[0, c, N : N + 8]
        for k in range(1, nz):
            a = got[k, c, N : N + 8]
            top = top * a[0:1] + got[k, c, 0:N]
            keep = keep * a
        tops[y, c, 0:N] = top
        tops[y, c, N : N + 8] = keep
        for i in range(1, ny):
            y_copy(c, i).start()

    def stage_b(c):
        for i in range(1, ny):
            y_copy(c, i).wait_recv()
        enter = jnp.zeros((N, 2 * P_SIZE), F32)
        last = enter
        for k in range(ny):
            a = tops[k, c, N : N + 1]
            top = tops[k, c, 0:N]
            enter = jnp.where(k < y, enter * a + top, enter)
            last = last * a + top
        for k in range(nz):
            staged[k, c] = enter
            if k < nz - 1:
                enter = enter * got[k, c, N : N + 1] + got[k, c, 0:N]
        for i in range(1, nz):
            e_copy(c, i).start()
        e_ref[CH * z + c] = staged[z, c]
        turned[c] = last.T

        @pl.when(away)
        def _():
            swap_copy(c).start()

        @pl.when(jnp.logical_not(away))
        def _():
            g_ref[c, y, core, zl, z] = turned[c, pl.ds(32 * y, 32)]

    def stage_c(c):
        @pl.when(away)
        def _():
            swap_copy(c).wait_recv()

        for i in range(1, nz):
            fz_copy(c, i).start()

    def stage_d(c):
        for i in range(1, nz):
            fz_copy(c, i).wait_recv()
        fl_copy(c).start()

    def stage_e(c):
        fl_copy(c).wait_recv()
        for i in range(1, ny):
            fy_copy(c, i).start()
        fc_copy(c, 0).start()

    def stage_f(c):
        for i in range(1, ny):
            fy_copy(c, i).wait_recv()
            fc_copy(c, i).start()

    stages = (stage_a, stage_b, stage_c, stage_d, stage_e, stage_f)
    for step in range(CH + len(stages) - 1):
        for n, stage in enumerate(stages):
            if 0 <= step - n < CH:
                stage(step - n)

    for c in range(CH):
        for i in range(1, nz):
            e_copy(c, i).wait_recv()
            z_copy(c, i).wait_send()
            e_copy(c, i).wait_send()
            fz_copy(c, i).wait_send()
        for i in range(1, ny):
            y_copy(c, i).wait_send()
            fy_copy(c, i).wait_send()
        for i in range(ny):
            fc_copy(c, i).wait()
        fl_copy(c).wait_send()

        @pl.when(away)
        def _():
            swap_copy(c).wait_send()


def scan(s_ext, nz, ny):
    pairs = s_ext.shape[0]
    dma = pltpu.SemaphoreType.DMA
    vmem = pl.BlockSpec(memory_space=pltpu.VMEM)
    return pl.pallas_call(
        functools.partial(scan_kernel, (nz, ny)),
        out_shape=(
            jax.ShapeDtypeStruct((pairs, N, 2 * P_SIZE), F32),
            jax.ShapeDtypeStruct((CH, ny, 2, 2, nz, 32, N), F32),
        ),
        in_specs=[vmem],
        out_specs=(vmem, vmem),
        scratch_shapes=[
            pltpu.VMEM((nz, CH, N + 8, 2 * P_SIZE), F32),
            pltpu.VMEM((ny, CH, N + 8, 2 * P_SIZE), F32),
            pltpu.VMEM((nz, CH, N, 2 * P_SIZE), F32),
            pltpu.VMEM((CH, 2 * P_SIZE, N), F32),
            dma((CH, 3)), dma((CH, 3)),
            dma((CH, 3)), dma((CH, 3)),
            dma((CH, 3)), dma((CH, 3)),
            dma((CH,)), dma((CH,)),
            dma((CH, 3)), dma((CH, 3)),
            dma((CH,)), dma((CH,)),
            dma((CH, 3)), dma((CH, 3)),
            dma((CH, 4)), dma((CH, 4)),
        ],
        compiler_params=pltpu.CompilerParams(
            collective_id=0, has_side_effects=True, vmem_limit_bytes=24 * MIB
        ),
        name="scan",
    )(s_ext)


def decode_kernel(
    row_ref, slot_ref, g_ref, x_ref, b_ref, c_ref, d_ref, spread_ref, out_ref, cache_ref, coef
):
    chunk = pl.program_id(0)
    rows = x_ref.shape[1]
    heads = d_ref.shape[2]
    half = heads // 2
    spread = spread_ref[...]

    @pl.when(chunk == 0)
    def _():
        lane = lax.broadcasted_iota(jnp.int32, (STEPS * STEPS, heads), 1)
        for r in range(rows):
            keep = d_ref[:, r, :]
            b = b_ref[:, r, :].astype(F32)
            c = c_ref[:, r, :].astype(F32)
            grid = []
            for k in range(STEPS):
                line = [jnp.zeros((1, heads), F32)] * k + [jnp.ones((1, heads), F32)]
                for s in range(k + 1, STEPS):
                    line.append(line[-1] * keep[s : s + 1])
                grid.append(jnp.concatenate(line, axis=0))
            line = [keep[0:1]]
            for s in range(1, STEPS):
                line.append(line[-1] * keep[s : s + 1])
            reach = jnp.concatenate(grid, axis=0)
            meet = []
            for g in range(2):
                bg, cg = b[:, g * N : (g + 1) * N], c[:, g * N : (g + 1) * N]
                meet.append(
                    jnp.concatenate(
                        [jnp.sum(cg * bg[k : k + 1], axis=1, keepdims=True) for k in range(STEPS)],
                        axis=0,
                    )
                )
            met = reach * jnp.where(lane < half, meet[0], meet[1])
            tail = [grid[k][STEPS - 1 : STEPS] for k in range(STEPS)]
            table = jnp.concatenate([met] + line + tail, axis=0)
            coef[r] = jnp.concatenate([table, table], axis=1)

    for zi in range(4):
        g = zi // 2
        at = pl.ds(pl.multiple_of((4 * zi + chunk) * 2 * P_SIZE, 2 * P_SIZE), 2 * P_SIZE)
        sp = spread_ref[:, at]
        for r in range(rows):
            prompt = row_ref[r]
            f = g_ref[0, :, prompt % 2, prompt // 2, zi].reshape(2 * P_SIZE, N)
            b = b_ref[:, r, g * N : (g + 1) * N]
            c = c_ref[:, r, g * N : (g + 1) * N]
            x = x_ref[:, r, at].astype(F32)
            co = split_spread(coef[r], sp)
            f_hi = f.astype(BF16)
            f_low = (f - f_hi.astype(F32)).astype(BF16)
            seen = dot(c, f_hi, ((1,), (1,))) + dot(c, f_low, ((1,), (1,)))
            base = STEPS * STEPS
            answer = seen * co[base : base + STEPS]
            for k in range(STEPS):
                answer += co[k * STEPS : (k + 1) * STEPS] * x[k : k + 1]
            out_ref[:, r, at] = answer.astype(BF16)
            push = x * co[base + STEPS : base + 2 * STEPS]
            p_hi = push.astype(BF16).astype(F32)
            both = jnp.concatenate([p_hi, push - p_hi], axis=0)
            bb = jnp.concatenate([b, b], axis=0).astype(F32)
            gain = dot(both.T.astype(BF16), bb.astype(BF16))
            kept = jnp.broadcast_to(co[base + STEPS - 1 : base + STEPS], (2 * P_SIZE, N)).T
            cache_ref[slot_ref[r], zi, 0] = (f * kept + gain).astype(BF16)


def decode(row_prompt, cache_slot, g, x, b, c, keep, spread):
    rows = x.shape[1]
    heads = keep.shape[2]
    nz = g.shape[4]
    smem = pl.BlockSpec(memory_space=pltpu.SMEM)

    def whole(a):
        return pl.BlockSpec(a.shape, lambda i: (0,) * a.ndim)

    out, cache = pl.pallas_call(
        decode_kernel,
        grid=(CH,),
        out_shape=(
            jax.ShapeDtypeStruct(x.shape, BF16),
            jax.ShapeDtypeStruct((rows, nz, CH, 2 * P_SIZE, N), BF16),
        ),
        in_specs=[
            smem,
            smem,
            pl.BlockSpec((1,) + g.shape[1:], lambda i: (i, 0, 0, 0, 0, 0, 0)),
            whole(x),
            whole(b),
            whole(c),
            whole(keep),
            whole(spread),
        ],
        out_specs=(
            whole(x),
            pl.BlockSpec((rows, nz, 1, 2 * P_SIZE, N), lambda i: (0, 0, i, 0, 0)),
        ),
        scratch_shapes=[pltpu.VMEM((rows, STEPS * STEPS + 2 * STEPS, 2 * heads), F32)],
        compiler_params=pltpu.CompilerParams(
            dimension_semantics=("arbitrary",), vmem_limit_bytes=24 * MIB
        ),
        name="decode",
    )(row_prompt, cache_slot, g, x, b, c, keep, spread)
    return out, cache.reshape(rows, heads, P_SIZE, N)


def per_device(x, b, c, decay, row_prompt, cache_slot, step_x, step_b, step_c, step_decay):
    x, b, c, decay = x[0], b[0], c[0], decay[0]
    length, wide = x.shape
    heads = decay.shape[0]
    pairs = heads // 2
    spread = spread_matrix(heads)
    nz, ny = 4, lax.axis_size("seq") // 4

    def rows(a):
        return pl.BlockSpec((B, a.shape[1]), lambda i: (i, 0))

    def whole(a):
        return pl.BlockSpec(a.shape, lambda i: (0,) * a.ndim)

    lanes = pl.BlockSpec((heads, B), lambda i: (0, i))
    params = pltpu.CompilerParams(
        dimension_semantics=("arbitrary",), vmem_limit_bytes=32 * MIB
    )
    part, s_ext = pl.pallas_call(
        prep_kernel,
        grid=(length // B,),
        out_shape=(
            jax.ShapeDtypeStruct(x.shape, BF16),
            jax.ShapeDtypeStruct((pairs, N + 8, 2 * P_SIZE), F32),
        ),
        in_specs=[rows(x), rows(b), rows(c), lanes, whole(spread)],
        out_specs=(rows(x), pl.BlockSpec((pairs, N + 8, 2 * P_SIZE), lambda i: (0, 0, 0))),
        scratch_shapes=[pltpu.VMEM((N, wide), F32), pltpu.VMEM((8, 2 * heads), F32)],
        compiler_params=params,
        name="prep",
    )(x, b, c, decay, spread)
    enter, finals = scan(s_ext, nz, ny)
    seq_output = pl.pallas_call(
        close_kernel,
        grid=(length // B,),
        out_shape=jax.ShapeDtypeStruct(x.shape, BF16),
        in_specs=[rows(x), rows(c), lanes, whole(enter), whole(spread)],
        out_specs=rows(x),
        scratch_shapes=[pltpu.VMEM((N, wide), BF16), pltpu.VMEM((8, 2 * heads), F32)],
        compiler_params=params,
        name="close",
    )(part, c, decay, enter, spread)
    step_output, state_cache = decode(
        row_prompt, cache_slot, finals, step_x, step_b, step_c, step_decay, spread
    )
    return seq_output[None], step_output, state_cache


def solution(mesh):
    return jax.shard_map(
        per_device,
        mesh=mesh,
        in_specs=(
            P("tp", "seq", "dp"),
            P("tp", "seq", "dp"),
            P("tp", "seq", "dp"),
            P("tp", "dp", "seq"),
            P(("seq", "dp")),
            P(("seq", "dp")),
            P(None, ("seq", "dp"), "tp"),
            P(None, ("seq", "dp"), "tp"),
            P(None, ("seq", "dp"), "tp"),
            P(None, ("seq", "dp"), "tp"),
        ),
        out_specs=(
            P("tp", "seq", "dp"),
            P(None, ("seq", "dp"), "tp"),
            P(("seq", "dp"), "tp", None, None),
        ),
        check_vma=False,
    )
```

time: 660 us -> 135 us (0.20)
  waiting for transfers between devices: 377 us -> 0 us
  Pallas kernels: 0 us -> 126 us
  matrix products: 95 us -> 0 us
  local copies, waits for them, and re-layouts: 81.9 us -> 6.16 us
  other arithmetic: 43.2 us -> 0 us
  blocking collectives: 39.7 us -> 0 us
  between operations: 14.7 us -> 0.74 us
    psum x1 -> x0, waiting for transfers between devices: 191 us -> none  [from_root(): return lax.psum(block, axis)]
    all_gather x2 -> x0, waiting for transfers between devices: 186 us -> none  [the longest x1 154 us: prefix(): gathered = jax.tree.map(lambda a: lax.all_gather(a, axis), part)]
    pallas_call x0 -> x4, Pallas kernels: none -> 126 us  [the longest x1 86.1 us: scan(): pl.pallas_call(functools.partial(scan_kernel, (nz, ny)), out_shape=(jax.S...]
    dot_general x18 -> x0, matrix products: 95 us -> none  [the longest x8 65.7 us: per_device(): jnp.einsum('rghpn,rgn->rghp', state, c_group, precision=HIGH)]
    all_gather x1 -> x0, blocking collectives: 39.7 us -> none  [prefix(): gathered = jax.tree.map(lambda a: lax.all_gather(a, axis), part)]
    unnamed x106 -> x26, local copies, waits for them, and re-layouts: 42.6 us -> 6.16 us
    convert_element_type x4 -> x0, other arithmetic: 19.3 us -> none  [the longest x1 15 us: per_device(): finished = state.astype(jnp.bfloat16).reshape(rows, dec_heads, P_SIZE, N)]
    add x5 -> x0, other arithmetic: 12.9 us -> none  [the longest x1 7.23 us: per_device(): keep[..., None, None] * state]
  transfers between devices with their start and end apart: 4 -> 0, of which waited for: 3 -> 0; matrix products, arithmetic and copies ran while one was open for 12% -> 0% of each run, Pallas kernels for 0% -> 0%
where the time goes in v1:
time: 135 us; the launch traced here: 133 us
  Pallas kernels  126 us (93%)
  local copies, waits for them, and re-layouts  6.16 us (5%)
    pallas_call x1, Pallas kernels, scan(): pl.pallas_call(functools.partial(scan_kernel, (nz, ny)), out_shape=(jax.S...  86.1 us
    pallas_call x1, Pallas kernels, decode(): pl.pallas_call(decode_kernel, grid=(CH,), out_shape=(jax.ShapeDtypeStruct...  17.8 us
    pallas_call x1, Pallas kernels, per_device(): pl.pallas_call(prep_kernel, grid=(length // B,), out_shape=(jax.ShapeDtyp...  15.5 us
    pallas_call x1, Pallas kernels, per_device(): pl.pallas_call(close_kernel, grid=(length // B,), out_shape=jax.ShapeDtyp...  6.56 us
    unnamed x26, local copies, waits for them, and re-layouts  6.16 us

profile of v1, /device:TPU:7, one launch (start us, length us, event | category | flops | bytes accessed | tf_op | source)
XLA Modules:
  0.0 132.9 jit_solution(8694967352532935171)
XLA Ops:
  0.6 0.0 copy-start
  0.6 2.2 %copy-done = bf16[1,1024,2048]{2,1,0:T(8,128)(2,1)S(1)} copy-done((bf16[1,1024,2048]{2,1,0:T(8,128)(2,1)S(1)}, bf16[1,1024,2048]{2,1,0:T(8,128)(2,1)}, u32[]{:S(2)}) %copy-start) | copy-done | bytes 4194328
  2.8 0.0 copy-start.1
  2.8 0.9 copy-done.1
  3.8 0.0 copy-start.3
  3.8 1.0 copy-done.3
  4.8 0.0 copy-start.5
  4.8 0.9 copy-done.5
  5.7 0.0 copy-start.6
  5.7 1.0 copy-done.6
  6.8 0.0 copy-start.2
  6.8 0.0 copy-start.4
  6.8 15.5 %prep.1 = (bf16[1024,2048]{1,0:T(8,128)(2,1)S(1)}, f32[16,136,128]{2,1,0:T(8,128)S(1)}) custom-call(bf16[1024,2048]{1,0:T(8,128)(2,1)S(1)} %bitcast.6, bf16[1024,256]{1,0:T(8,128)(2,1)S(1)} %bitcast.11, bf16[1024,256]{1,0:T(8,128)(2,1)S(1)} %bitcast.7, f32[32,1024]{1,0:T(8,128)S(1)} %bitcast.9, bf16[64,2048]{1,0:T(8,128)(2,1)S(1)} %copy-done.1), custom_call_target="tpu_custom_call" | custom-call | tf_op jit(solution)/shard_map/prep/pallas_call | solution.py:486
  22.3 86.1 %scan.1 = (f32[16,128,128]{2,1,0:T(8,128)S(1)}, f32[4,4,2,2,4,32,128]{6,5,4,3,2,1,0:T(8,128)S(1)}) custom-call(f32[16,136,128]{2,1,0:T(8,128)S(1)} %get-tuple-element.10.s_ref), custom_call_target="tpu_custom_call" | custom-call | tf_op jit(solution)/shard_map/scan/pallas_call | solution.py:332
  108.4 0.0 copy-done.2
  108.4 0.0 copy-done.4
  108.4 0.0 copy-start.7
  108.4 0.0 copy-start.8
  108.4 0.0 copy-start.9
  108.4 0.0 copy-start.10
  108.4 0.0 copy-start.11
  108.4 0.0 copy-start.12
  108.5 6.6 %close.1 = bf16[1024,2048]{1,0:T(8,128)(2,1)} custom-call(bf16[1024,2048]{1,0:T(8,128)(2,1)S(1)} %get-tuple-element.9.y_ref, bf16[1024,256]{1,0:T(8,128)(2,1)S(1)} %bitcast.8, f32[32,1024]{1,0:T(8,128)S(1)} %bitcast.10, f32[16,128,128]{2,1,0:T(8,128)S(1)} %get-tuple-element.11.e_ref, bf16[64,2048]{1,0:T(8,128)(2,1)S(1)} %copy-done.2), custom_call_target="tpu_custom_call" | custom-call | tf_op jit(solution)/shard_map/close/pallas_call | solution.py:500
  115.0 0.0 copy-done.7
  115.0 0.0 copy-done.8
  115.0 0.0 copy-done.9
  115.0 0.0 copy-done.10
  115.0 0.0 copy-done.11
  115.1 0.0 copy-done.12
  115.1 17.8 %decode.1 = (bf16[8,4,2048]{2,1,0:T(4,128)(2,1)}, bf16[4,4,4,128,128]{4,3,2,1,0:T(8,128)(2,1)}) custom-call(s32[4]{0:T(128)S(1)} %copy-done.11, s32[4]{0:T(128)S(1)} %copy-done.12, f32[4,4,2,2,4,32,128]{6,5,4,3,2,1,0:T(8,128)S(1)} %get-tuple-element.12.g_ref, bf16[8,4,2048]{2,1,0:T(4,128)(2,1)S(1)} %copy-done.7, bf16[8,4,256]{2,1,0:T(4,128)(2,1)S(1)} %copy-done.8, ...), custom_call_target="tpu_custom_call" | custom-call | tf_op jit(solution)/shard_map/decode/pallas_call | solution.py:438
Async XLA Ops:
  0.6 2.2 %copy-start = (bf16[1,1024,2048]{2,1,0:T(8,128)(2,1)S(1)}, bf16[1,1024,2048]{2,1,0:T(8,128)(2,1)}, u32[]{:S(2)}) copy-start(bf16[1,1024,2048]{2,1,0:T(8,128)(2,1)} %param.11) | copy-start | bytes 12582916
  2.8 0.9 copy-start.1
  3.8 1.0 copy-start.3
  4.8 0.9 copy-start.5
  5.7 1.0 copy-start.6
  6.8 101.6 %copy-start.2 = (bf16[64,2048]{1,0:T(8,128)(2,1)S(1)}, bf16[64,2048]{1,0:T(8,128)(2,1)}, u32[]{:S(2)}) copy-start(bf16[64,2048]{1,0:T(8,128)(2,1)} %constant.2.clone.spread_ref) | copy-start | bytes 786436
  6.8 101.6 %copy-start.4 = (bf16[1,1024,256]{2,1,0:T(8,128)(2,1)S(1)}, bf16[1,1024,256]{2,1,0:T(8,128)(2,1)}, u32[]{:S(2)}) copy-start(bf16[1,1024,256]{2,1,0:T(8,128)(2,1)} %param.13) | copy-start | bytes 1572868
  108.4 6.6 %copy-start.7 = (bf16[8,4,2048]{2,1,0:T(4,128)(2,1)S(1)}, bf16[8,4,2048]{2,1,0:T(4,128)(2,1)}, u32[]{:S(2)}) copy-start(bf16[8,4,2048]{2,1,0:T(4,128)(2,1)} %x_ref.1) | copy-start | bytes 393220
  108.4 6.6 %copy-start.8 = (bf16[8,4,256]{2,1,0:T(4,128)(2,1)S(1)}, bf16[8,4,256]{2,1,0:T(4,128)(2,1)}, u32[]{:S(2)}) copy-start(bf16[8,4,256]{2,1,0:T(4,128)(2,1)} %b_ref.1) | copy-start | bytes 49156
  108.4 6.6 %copy-start.9 = (bf16[8,4,256]{2,1,0:T(4,128)(2,1)S(1)}, bf16[8,4,256]{2,1,0:T(4,128)(2,1)}, u32[]{:S(2)}) copy-start(bf16[8,4,256]{2,1,0:T(4,128)(2,1)} %c_ref.1) | copy-start | bytes 49156
  108.4 6.6 %copy-start.10 = (f32[8,4,32]{2,1,0:T(4,128)S(1)}, f32[8,4,32]{2,1,0:T(4,128)}, u32[]{:S(2)}) copy-start(f32[8,4,32]{2,1,0:T(4,128)} %d_ref.1) | copy-start | bytes 12292
  108.4 6.6 %copy-start.11 = (s32[4]{0:T(128)S(1)}, s32[4]{0:T(128)}, u32[]{:S(2)}) copy-start(s32[4]{0:T(128)} %row_ref.1) | copy-start | bytes 52
  108.4 6.6 %copy-start.12 = (s32[4]{0:T(128)S(1)}, s32[4]{0:T(128)}, u32[]{:S(2)}) copy-start(s32[4]{0:T(128)} %slot_ref.1) | copy-start | bytes 52

commit v2 on v1

v2 whole, which is shorter than its diff:
```python
import functools
import math

import jax
import jax.numpy as jnp
from jax import lax
from jax.experimental import pallas as pl
from jax.experimental.pallas import tpu as pltpu
from jax.sharding import PartitionSpec as P

MESH = pl.DeviceIdType.MESH
P_SIZE = 64
N = 128
B = 128
STEPS = 8
LOG2E = math.log2(math.e)
HIGH = lax.Precision.HIGHEST
F32 = jnp.float32
BF16 = jnp.bfloat16
CH = 4
MIB = 2**20


def dot(a, b, dims=((1,), (0,)), precision=None):
    return lax.dot_general(
        a, b, (dims, ((), ())), preferred_element_type=F32, precision=precision
    )


def spread_matrix(shape):
    heads = shape[0] // 2
    row = lax.broadcasted_iota(jnp.int32, shape, 0)
    lane = lax.broadcasted_iota(jnp.int32, shape, 1)
    return (row % heads == lane // P_SIZE).astype(F32).astype(BF16)


def pair_lanes(pair):
    return pl.ds(pl.multiple_of(pair * 2 * P_SIZE, 2 * P_SIZE), 2 * P_SIZE)


def hi_low(v):
    hi = v.astype(BF16)
    lane = lax.broadcasted_iota(jnp.int32, v.shape, 1)
    return jnp.where(lane < v.shape[1] // 2, hi, (v - hi.astype(F32)).astype(BF16))


def decode_tables(x_ref, b_ref, c_ref, d_ref, spread_ref, pre_ref, reach_ref, push_ref, last_ref, cc_ref, bb_ref):
    rows, heads = d_ref.shape[1], d_ref.shape[2]
    lane = lax.broadcasted_iota(jnp.int32, (STEPS * STEPS, heads), 1)
    x_all = x_ref[...].astype(F32)
    b_all = b_ref[...].astype(F32)
    c_all = c_ref[...].astype(F32)
    pushes, cs, bs = [], [], []
    for r in range(rows):
        keep = d_ref[:, r, :]
        x, b, c = x_all[:, r, :], b_all[:, r, :], c_all[:, r, :]
        grid = []
        for k in range(STEPS):
            line = [jnp.zeros((1, heads), F32)] * k + [jnp.ones((1, heads), F32)]
            for s in range(k + 1, STEPS):
                line.append(line[-1] * keep[s : s + 1])
            grid.append(jnp.concatenate(line, axis=0))
        line = [keep[0:1]]
        for s in range(1, STEPS):
            line.append(line[-1] * keep[s : s + 1])
        meet = []
        for g in range(2):
            bg, cg = b[:, g * N : (g + 1) * N], c[:, g * N : (g + 1) * N]
            meet.append(
                jnp.concatenate(
                    [jnp.sum(cg * bg[k : k + 1], axis=1, keepdims=True) for k in range(STEPS)],
                    axis=0,
                )
            )
        met = jnp.concatenate(grid, axis=0) * jnp.where(lane < heads // 2, meet[0], meet[1])
        left = [grid[k][STEPS - 1 : STEPS] for k in range(STEPS)]
        table = jnp.concatenate([met] + line + left, axis=0)
        co = dot(hi_low(jnp.concatenate([table, table], axis=1)), spread_ref[...])
        base = STEPS * STEPS
        local = co[0:STEPS] * x[0:1]
        for k in range(1, STEPS):
            local += co[k * STEPS : (k + 1) * STEPS] * x[k : k + 1]
        pre_ref[r] = local
        reach_ref[r] = co[base : base + STEPS]
        push = x * co[base + STEPS : base + 2 * STEPS]
        hi = push.astype(BF16).astype(F32)
        pushes += [hi, push - hi]
        last_ref[r] = jnp.broadcast_to(line[-1], (N, heads)).T
        cs.append(c)
        bs.append(b)
    pushes = jnp.concatenate(pushes, axis=0)
    for pair in range(heads // 2):
        at = pl.ds(pair * 2 * P_SIZE, 2 * P_SIZE)
        push_ref[at, :] = pushes[:, pair * 2 * P_SIZE : (pair + 1) * 2 * P_SIZE].T.astype(BF16)
    cs = jnp.concatenate(cs, axis=0).astype(BF16)
    for g in range(2):
        cg = cs[:, g * N : (g + 1) * N]
        cc_ref[g] = jnp.concatenate([cg, cg], axis=1)
        lines = []
        for r in range(rows):
            b = bs[r][:, g * N : (g + 1) * N]
            zero = jnp.zeros((2 * STEPS, N), F32)
            mine = jnp.concatenate([b, b], axis=0)
            lines.append(
                jnp.concatenate([mine if q == r else zero for q in range(rows)], axis=1)
            )
        bb_ref[g] = jnp.concatenate(lines, axis=0).astype(BF16)


def core_kernel(
    sizes,
    x_hbm,
    b_hbm,
    c_hbm,
    d_hbm,
    sx_hbm,
    sb_hbm,
    sc_hbm,
    sd_hbm,
    out_hbm,
    g_hbm,
    pre_hbm,
    reach_hbm,
    push_hbm,
    last_hbm,
    cc_hbm,
    bb_hbm,
    xv,
    bv,
    cv,
    dv,
    sx_ref,
    sb_ref,
    sc_ref,
    sd_ref,
    out_ref,
    g_ref,
    pre_ref,
    reach_ref,
    push_ref,
    last_ref,
    cc_ref,
    bb_ref,
    spread_ref,
    bt,
    part,
    state,
    cum,
    cum_t,
    grown,
    remain,
    s_ref,
    e_ref,
    got,
    tops,
    staged,
    turned,
    x_sem,
    in_sem,
    out_sem,
    g_sem,
    table_sem,
    z_send,
    z_recv,
    y_send,
    y_recv,
    e_send,
    e_recv,
    fz_send,
    fz_recv,
    fl_send,
    fl_recv,
    fy_send,
    fy_recv,
    fc_send,
    fc_recv,
):
    nz, ny = sizes
    length, wide = xv.shape
    heads = dv.shape[0]
    groups = bv.shape[1] // N
    per = heads // groups
    blocks = length // B
    s, t, d = lax.axis_index("seq"), lax.axis_index("tp"), lax.axis_index("dp")
    y, z = s // nz, s % nz
    zl, core = d // 2, d % 2
    away = t != d

    def x_load(pair):
        at = pair_lanes(pair)
        return pltpu.make_async_copy(x_hbm.at[:, at], xv.at[:, at], x_sem.at[pair])

    loads = [
        pltpu.make_async_copy(src, dst, in_sem.at[n])
        for n, (src, dst) in enumerate(
            (
                (d_hbm, dv), (b_hbm, bv), (c_hbm, cv), (sx_hbm, sx_ref), (sb_hbm, sb_ref),
                (sc_hbm, sc_ref), (sd_hbm, sd_ref),
            )
        )
    ]
    tables = [
        pltpu.make_async_copy(src, dst, table_sem.at[n])
        for n, (src, dst) in enumerate(
            (
                (pre_ref, pre_hbm), (reach_ref, reach_hbm), (push_ref, push_hbm),
                (last_ref, last_hbm), (cc_ref, cc_hbm), (bb_ref, bb_hbm),
            )
        )
    ]

    def y_store(pair):
        at = pair_lanes(pair)
        return pltpu.make_async_copy(out_ref.at[:, at], out_hbm.at[:, at], out_sem.at[pair])

    def g_store(c):
        return pltpu.make_async_copy(g_ref.at[c], g_hbm.at[c], g_sem.at[c])

    loads[0].start()
    loads[1].start()
    for c in range(CH):
        for q in range(nz):
            x_load(CH * q + c).start()
    for load in loads[2:]:
        load.start()
    spread_ref[...] = spread_matrix(spread_ref.shape)

    def z_dev(i):
        return (y * nz + (z + i) % nz, t, d)

    def y_dev(i):
        return (((y + i) % ny) * nz + z, t, d)

    def cross_dev(i):
        return (y * nz + (z + i) % nz, d, t)

    zl_dev = (s, t, (1 - zl) * 2 + core)
    core_dev = (s, t, zl * 2 + 1 - core)

    barrier = pltpu.get_barrier_semaphore()
    others = [z_dev(i) for i in range(1, nz)] + [y_dev(i) for i in range(1, ny)]
    others += [zl_dev, core_dev]
    for dev in others:
        pl.semaphore_signal(barrier, inc=1, device_id=dev, device_id_type=MESH)

    @pl.when(away)
    def _():
        for i in range(nz):
            pl.semaphore_signal(barrier, inc=1, device_id=cross_dev(i), device_id_type=MESH)

    pl.semaphore_wait(barrier, jnp.where(away, len(others) + nz, len(others)))

    def copy(src, dst, send, recv, dev):
        return pltpu.make_async_remote_copy(
            src_ref=src, dst_ref=dst, send_sem=send, recv_sem=recv, device_id=dev,
            device_id_type=MESH,
        )

    def z_copy(c, i):
        return copy(
            s_ref.at[CH * ((z + i) % nz) + c], got.at[z, c], z_send.at[c, i - 1],
            z_recv.at[c, i - 1], z_dev(i),
        )

    def y_copy(c, i):
        return copy(
            tops.at[y, c], tops.at[y, c], y_send.at[c, i - 1], y_recv.at[c, i - 1], y_dev(i)
        )

    def e_copy(c, i):
        return copy(
            staged.at[(z + i) % nz, c], e_ref.at[CH * z + c], e_send.at[c, i - 1],
            e_recv.at[c, i - 1], z_dev(i),
        )

    def fz_copy(c, i):
        return copy(
            turned.at[c, pl.ds(32 * y, 32)], g_ref.at[c, y, t % 2, t // 2, z], fz_send.at[c, i],
            fz_recv.at[c, i], cross_dev(i),
        )

    def fl_copy(c):
        ref = g_ref.at[c, y, core, zl]
        return copy(ref, ref, fl_send.at[c], fl_recv.at[c], zl_dev)

    def fy_copy(c, i, other):
        ref = g_ref.at[c, y, core, 1 - zl if other else zl]
        n = 3 * other + i - 1
        return copy(ref, ref, fy_send.at[c, n], fy_recv.at[c, n], y_dev(i))

    def fc_copy(c, i):
        ref = g_ref.at[c, (y + ny - i) % ny, core]
        return copy(ref, ref, fc_send.at[c, i], fc_recv.at[c, i], core_dev)

    loads[0].wait()
    row = lax.broadcasted_iota(jnp.int32, (B, B), 0)
    col = lax.broadcasted_iota(jnp.int32, (B, B), 1)
    upper = (row <= col).astype(F32)
    lead = jnp.zeros((1, 2 * heads), F32)
    leads = []
    for k in range(blocks):
        at = pl.ds(k * B, B)
        dec = dv[:, at]
        sums = dot(jnp.concatenate([dec, dec], axis=0) * LOG2E, upper, precision=HIGH)
        cum[:, at] = sums
        cum_t[at, :] = sums.T
        leads.append(lead)
        lead = lead + cum_t[k * B + B - 1 : k * B + B, :]
    for k in range(blocks):
        at = pl.ds(k * B, B)
        whole = cum_t[at, :] + leads[k]
        grown[at, :] = hi_low(jnp.exp2(whole))
        remain[at, :] = hi_low(jnp.exp2(jnp.minimum(lead - whole, 0.0)))
    keep = hi_low(jnp.broadcast_to(jnp.exp2(lead), (16, 2 * heads)))

    loads[1].wait()
    for k in range(blocks):
        for g in range(groups):
            at = pl.ds(k * B, B)
            bt[g, :, at] = bv[at, g * N : (g + 1) * N].T

    def own_state(c, carry):
        left = remain[...]
        for q in range(nz):
            pair = CH * q + c
            g = q * CH * 2 // per
            x_load(pair).wait()
            at = pair_lanes(pair)
            sp = spread_ref[:, at]
            scaled = (xv[:, at].astype(F32) * dot(left, sp)).astype(BF16)
            s_ref[pair, 0:N] = dot(bt[g], scaled)
            s_ref[pair, N : N + 8] = dot(keep, sp)[0:8]
        for i in range(1, nz):
            z_copy(c, i).start()
        got[z, c] = s_ref[CH * z + c]
        return carry

    with jax.named_scope("own_state"):
        lax.fori_loop(0, CH, own_state, 0)
    for load in loads[2:]:
        load.wait()
    with jax.named_scope("decode_tables"):
        decode_tables(
            sx_ref, sb_ref, sc_ref, sd_ref, spread_ref, pre_ref, reach_ref, push_ref, last_ref,
            cc_ref, bb_ref,
        )
    for table in tables:
        table.start()
    state[...] = jnp.zeros((N, wide), F32)
    lane = lax.broadcasted_iota(jnp.int32, (B, 2 * P_SIZE), 1)

    def block(k):
        rows = pl.ds(pl.multiple_of(k * B, B), B)
        sums, sums_t = cum[:, rows], cum_t[rows, :]
        last = sums_t[B - 1 : B, :]
        grow = hi_low(jnp.exp2(sums_t))
        left = hi_low(jnp.exp2(last - sums_t))
        fade = hi_low(jnp.broadcast_to(jnp.exp2(last), (16, 2 * heads)))
        for g in range(groups):
            lanes = pl.ds(g * per * P_SIZE, per * P_SIZE)
            sp = spread_ref[:, lanes]
            c = cv[rows, g * N : (g + 1) * N]
            x = xv[rows, lanes]
            before = state[:, lanes]
            carried = dot(c, before.astype(BF16)) * dot(grow, sp)
            scaled = (x.astype(F32) * dot(left, sp)).astype(BF16)
            term = dot(bt[g, :, rows], scaled)
            state[:, lanes] = before * dot(fade, sp)[0:1, :] + term
            scores = jnp.where(row >= col, dot(c, bt[g, :, rows]), 0.0)
            for n in range(per // 2):
                weights = []
                for h in (g * per + 2 * n, g * per + 2 * n + 1):
                    gap = jnp.minimum(sums_t[:, h : h + 1] - sums[h : h + 1, :], 0.0)
                    weights.append((scores * jnp.exp2(gap)).astype(BF16))
                here = slice(n * 2 * P_SIZE, (n + 1) * 2 * P_SIZE)
                zero = jnp.zeros((B, 2 * P_SIZE), BF16)
                both = jnp.concatenate(
                    [
                        jnp.where(lane < P_SIZE, x[:, here], zero),
                        jnp.where(lane < P_SIZE, zero, x[:, here]),
                    ],
                    axis=0,
                )
                inner = dot(jnp.concatenate(weights, axis=1), both)
                part[rows, pl.ds((g * per + 2 * n) * P_SIZE, 2 * P_SIZE)] = inner + carried[:, here]

    def stage_a(c):
        for i in range(1, nz):
            z_copy(c, i).wait_recv()
        top = got[0, c, 0:N]
        kept = got[0, c, N : N + 8]
        for k in range(1, nz):
            a = got[k, c, N : N + 8]
            top = top * a[0:1] + got[k, c, 0:N]
            kept = kept * a
        tops[y, c, 0:N] = top
        tops[y, c, N : N + 8] = kept
        for i in range(1, ny):
            y_copy(c, i).start()

    def stage_b(c):
        for i in range(1, ny):
            y_copy(c, i).wait_recv()
        enter = jnp.zeros((N, 2 * P_SIZE), F32)
        last = enter
        for k in range(ny):
            a = tops[k, c, N : N + 1]
            top = tops[k, c, 0:N]
            enter = jnp.where(k < y, enter * a + top, enter)
            last = last * a + top
        turned[c] = last.T

        @pl.when(away)
        def _():
            fz_copy(c, 0).start()

        @pl.when(jnp.logical_not(away))
        def _():
            g_ref[c, y, core, zl, z] = turned[c, pl.ds(32 * y, 32)]

        for i in range(1, nz):
            fz_copy(c, i).start()
        for k in range(nz):
            staged[k, c] = enter
            if k < nz - 1:
                enter = enter * got[k, c, N : N + 1] + got[k, c, 0:N]
        e_ref[CH * z + c] = staged[z, c]
        for i in range(1, nz):
            e_copy(c, i).start()

    def stage_c(c):
        @pl.when(away)
        def _():
            fz_copy(c, 0).wait_recv()

        for i in range(1, nz):
            fz_copy(c, i).wait_recv()
        fl_copy(c).start()
        for i in range(1, ny):
            fy_copy(c, i, 0).start()

    def stage_d(c):
        fl_copy(c).wait_recv()
        for i in range(1, ny):
            fy_copy(c, i, 1).start()
        fc_copy(c, 0).start()

    def stage_e(c):
        for i in range(1, ny):
            fy_copy(c, i, 0).wait_recv()
            fy_copy(c, i, 1).wait_recv()
            fc_copy(c, i).start()

    def stage_f(c):
        for i in range(ny):
            fc_copy(c, i).wait_recv()
        g_store(c).start()

    def close(c):
        for i in range(1, nz):
            e_copy(c, i).wait_recv()
        for q in range(nz):
            pair = CH * q + c
            g = q * CH * 2 // per
            at = pair_lanes(pair)
            carried = dot(cv[:, g * N : (g + 1) * N], e_ref[pair].astype(BF16))
            carried = carried * dot(grown[...], spread_ref[:, at])
            out_ref[:, at] = (part[:, at] + carried).astype(BF16)
            y_store(pair).start()

    stages = (
        (stage_a, 0), (stage_b, 1), (stage_c, 2), (stage_d, 3), (stage_e, 4), (stage_f, 5),
        (close, CLOSE),
    )
    for k in range(EARLY):
        block(k)

    def step(n, carry):
        for stage, after in stages:

            @pl.when(jnp.logical_and(n >= after, n < after + CH))
            def _():
                with jax.named_scope(stage.__name__):
                    stage(n - after)

        @pl.when(n < blocks - EARLY)
        def _():
            with jax.named_scope("block"):
                block(n + EARLY)

        return carry

    lax.fori_loop(0, CLOSE + CH, step, 0)

    def drain(c, carry):
        for i in range(1, nz):
            z_copy(c, i).wait_send()
            e_copy(c, i).wait_send()
            fz_copy(c, i).wait_send()
        for i in range(1, ny):
            y_copy(c, i).wait_send()
            fy_copy(c, i, 0).wait_send()
            fy_copy(c, i, 1).wait_send()
        for i in range(ny):
            fc_copy(c, i).wait_send()
        g_store(c).wait()
        for q in range(nz):
            y_store(CH * q + c).wait()
        fl_copy(c).wait_send()

        @pl.when(away)
        def _():
            fz_copy(c, 0).wait_send()

        return carry

    with jax.named_scope("drain"):
        lax.fori_loop(0, CH, drain, 0)
        for table in tables:
            table.wait()


CLOSE = 6
EARLY = 2


def core(x, b, c, decay, sx, sb, sc, sd, nz, ny):
    length, wide = x.shape
    heads = decay.shape[0]
    pairs = heads // 2
    rows = sx.shape[1]
    dma = pltpu.SemaphoreType.DMA
    hbm = pl.BlockSpec(memory_space=pl.ANY)
    pair_shape = (N, 2 * P_SIZE)
    outs = (
        jax.ShapeDtypeStruct(x.shape, BF16),
        jax.ShapeDtypeStruct((CH, ny, 2, 2, nz, 32, N), F32),
        jax.ShapeDtypeStruct((rows, STEPS, wide), F32),
        jax.ShapeDtypeStruct((rows, STEPS, wide), F32),
        jax.ShapeDtypeStruct((wide, 2 * STEPS * rows), BF16),
        jax.ShapeDtypeStruct((rows, heads, N), F32),
        jax.ShapeDtypeStruct((2, rows * STEPS, 2 * N), BF16),
        jax.ShapeDtypeStruct((2, 2 * STEPS * rows, rows * N), BF16),
    )
    return pl.pallas_call(
        functools.partial(core_kernel, (nz, ny)),
        out_shape=outs,
        in_specs=[hbm] * 8,
        out_specs=(hbm,) * len(outs),
        scratch_shapes=[
            pltpu.VMEM(x.shape, BF16),
            pltpu.VMEM(b.shape, BF16),
            pltpu.VMEM(c.shape, BF16),
            pltpu.VMEM(decay.shape, F32),
            pltpu.VMEM(sx.shape, BF16),
            pltpu.VMEM(sb.shape, BF16),
            pltpu.VMEM(sc.shape, BF16),
            pltpu.VMEM(sd.shape, F32),
        ]
        + [pltpu.VMEM(out.shape, out.dtype) for out in outs]
        + [
            pltpu.VMEM((2 * heads, wide), BF16),
            pltpu.VMEM((2, N, length), BF16),
            pltpu.VMEM(x.shape, F32),
            pltpu.VMEM((N, wide), F32),
            pltpu.VMEM((2 * heads, length), F32),
            pltpu.VMEM((length, 2 * heads), F32),
            pltpu.VMEM((length, 2 * heads), BF16),
            pltpu.VMEM((length, 2 * heads), BF16),
            pltpu.VMEM((pairs, N + 8, 2 * P_SIZE), F32),
            pltpu.VMEM((pairs,) + pair_shape, F32),
            pltpu.VMEM((nz, CH, N + 8, 2 * P_SIZE), F32),
            pltpu.VMEM((ny, CH, N + 8, 2 * P_SIZE), F32),
            pltpu.VMEM((nz, CH) + pair_shape, F32),
            pltpu.VMEM((CH, 2 * P_SIZE, N), F32),
            dma((pairs,)),
            dma((7,)),
            dma((pairs,)),
            dma((CH,)),
            dma((6,)),
            dma((CH, 3)), dma((CH, 3)),
            dma((CH, 3)), dma((CH, 3)),
            dma((CH, 3)), dma((CH, 3)),
            dma((CH, 4)), dma((CH, 4)),
            dma((CH,)), dma((CH,)),
            dma((CH, 6)), dma((CH, 6)),
            dma((CH, 4)), dma((CH, 4)),
        ],
        compiler_params=pltpu.CompilerParams(
            collective_id=0, has_side_effects=True, vmem_limit_bytes=60 * MIB
        ),
        name="core",
    )(x, b, c, decay, sx, sb, sc, sd)


def decode_kernel(
    row_ref, slot_ref, y_in, g_ref, pre_ref, reach_ref, push_ref, last_ref, cc_ref, bb_ref,
    y_out, out_ref, cache_ref,
):
    chunk = pl.program_id(0)
    rows = pre_ref.shape[0]
    y_out[...] = y_in[...]

    for zi in range(4):
        g = zi // 2
        pair = CH * zi + chunk
        at = pair_lanes(pair)
        seen = []
        for prompt in range(4):
            f = g_ref[0, :, prompt % 2, prompt // 2, zi].reshape(2 * P_SIZE, N)
            hi = f.astype(BF16)
            low = (f - hi.astype(F32)).astype(BF16)
            seen.append(dot(cc_ref[g], jnp.concatenate([hi, low], axis=1), ((1,), (1,))))
        gain = dot(push_ref[at, :], bb_ref[g])
        for r in range(rows):
            mine = row_ref[r]
            pick = seen[0][r * STEPS : (r + 1) * STEPS]
            for prompt in range(1, 4):
                pick = jnp.where(mine == prompt, seen[prompt][r * STEPS : (r + 1) * STEPS], pick)
            out_ref[:, r, at] = (pick * reach_ref[r, :, at] + pre_ref[r, :, at]).astype(BF16)
            f = g_ref[0, :, mine % 2, mine // 2, zi].reshape(2 * P_SIZE, N)
            kept = jnp.concatenate(
                [
                    jnp.broadcast_to(last_ref[r, pl.ds(2 * pair + n, 1), :], (P_SIZE, N))
                    for n in range(2)
                ],
                axis=0,
            )
            cache_ref[slot_ref[r], zi, 0] = (f * kept + gain[:, r * N : (r + 1) * N]).astype(BF16)


def decode(row_prompt, cache_slot, y, g, tables, shape):
    rows = shape[1]
    nz = g.shape[4]
    heads = shape[2] // P_SIZE
    smem = pl.BlockSpec(memory_space=pltpu.SMEM)
    part = pl.BlockSpec((y.shape[0] // CH, y.shape[1]), lambda i: (i, 0))

    def whole(s):
        return pl.BlockSpec(s, lambda i: (0,) * len(s))

    seq, out, cache = pl.pallas_call(
        decode_kernel,
        grid=(CH,),
        out_shape=(
            jax.ShapeDtypeStruct(y.shape, BF16),
            jax.ShapeDtypeStruct(shape, BF16),
            jax.ShapeDtypeStruct((rows, nz, CH, 2 * P_SIZE, N), BF16),
        ),
        in_specs=[
            smem,
            smem,
            part,
            pl.BlockSpec((1,) + g.shape[1:], lambda i: (i, 0, 0, 0, 0, 0, 0)),
        ]
        + [whole(a.shape) for a in tables],
        out_specs=(
            part,
            whole(shape),
            pl.BlockSpec((rows, nz, 1, 2 * P_SIZE, N), lambda i: (0, 0, i, 0, 0)),
        ),
        compiler_params=pltpu.CompilerParams(
            dimension_semantics=("arbitrary",), vmem_limit_bytes=60 * MIB
        ),
        name="decode",
    )(row_prompt, cache_slot, y, g, *tables)
    return seq, out, cache.reshape(rows, heads, P_SIZE, N)


def per_device(x, b, c, decay, row_prompt, cache_slot, step_x, step_b, step_c, step_decay):
    nz, ny = 4, lax.axis_size("seq") // 4
    y, g, *tables = core(
        x[0], b[0], c[0], decay[0], step_x, step_b, step_c, step_decay, nz, ny
    )
    seq, out, cache = decode(row_prompt, cache_slot, y, g, tables, step_x.shape)
    return seq[None], out, cache


def solution(mesh):
    return jax.shard_map(
        per_device,
        mesh=mesh,
        in_specs=(
            P("tp", "seq", "dp"),
            P("tp", "seq", "dp"),
            P("tp", "seq", "dp"),
            P("tp", "dp", "seq"),
            P(("seq", "dp")),
            P(("seq", "dp")),
            P(None, ("seq", "dp"), "tp"),
            P(None, ("seq", "dp"), "tp"),
            P(None, ("seq", "dp"), "tp"),
            P(None, ("seq", "dp"), "tp"),
        ),
        out_specs=(
            P("tp", "seq", "dp"),
            P(None, ("seq", "dp"), "tp"),
            P(("seq", "dp"), "tp", None, None),
        ),
        check_vma=False,
    )
```

time: 135 us -> 101 us (0.75)
  Pallas kernels: 126 us -> 98.9 us
  local copies, waits for them, and re-layouts: 6.16 us -> 0 us
    pallas_call x3 -> x1, Pallas kernels: 108 us -> 91.1 us  [core(): pl.pallas_call(functools.partial(core_kernel, (nz, ny)), out_shape=outs,...]
    pallas_call x1, Pallas kernels: 17.8 us -> 7.76 us  [decode(): pl.pallas_call(decode_kernel, grid=(CH,), out_shape=(jax.ShapeDtypeStruct...]
    unnamed x26 -> x0, local copies, waits for them, and re-layouts: 6.16 us -> none
where the time goes in v2:
time: 101 us; the launch traced here: 99.5 us
  Pallas kernels  98.9 us (98%)
    pallas_call x1, Pallas kernels, core(): pl.pallas_call(functools.partial(core_kernel, (nz, ny)), out_shape=outs,...  91.1 us
    pallas_call x1, Pallas kernels, decode(): pl.pallas_call(decode_kernel, grid=(CH,), out_shape=(jax.ShapeDtypeStruct...  7.76 us

profile of v2, /device:TPU:7, one launch (start us, length us, event | category | flops | bytes accessed | tf_op | source)
XLA Modules:
  0.0 99.5 jit_solution(10152386408900255945)
XLA Ops:
  0.6 91.1 %core.1 = (bf16[1024,2048]{1,0:T(8,128)(2,1)}, f32[4,4,2,2,4,32,128]{6,5,4,3,2,1,0:T(8,128)}, f32[4,8,2048]{2,1,0:T(8,128)}, f32[4,8,2048]{2,1,0:T(8,128)}, bf16...) custom-call(bf16[1024,2048]{1,0:T(8,128)(2,1)} %bitcast.6, ...), custom_call_target="tpu_custom_call" | custom-call | tf_op jit(solution)/shard_map/core/pallas_call | solution.py:545
  91.8 7.8 %decode.1 = (bf16[1024,2048]{1,0:T(8,128)(2,1)}, bf16[8,4,2048]{2,1,0:T(4,128)(2,1)}, bf16[4,4,4,128,128]{4,3,2,1,0:T(8,128)(2,1)}) custom-call(s32[4]{0:T(128)} %row_ref.1, s32[4]{0:T(128)} %slot_ref.1, bf16[1024,2048]{1,0:T(8,128)(2,1)} %get-tuple-element.14.y_in, f32[4,4,2,2,4,32,128]{6,5,4,3,2,1,0:T(8,128)} %get-tuple-element.15.g_ref, ...), custom_call_target="tpu_custom_call" | custom-call | tf_op jit(solution)/shard_map/decode/pallas_call | solution.py:642

commit v3 on v2

--- a/solution.py
+++ b/solution.py
@@ -14,7 +14,6 @@
 B = 128
 STEPS = 8
 LOG2E = math.log2(math.e)
-HIGH = lax.Precision.HIGHEST
 F32 = jnp.float32
 BF16 = jnp.bfloat16
 CH = 4
@@ -151,25 +150,29 @@
     remain,
     s_ref,
     e_ref,
-    got,
+    first,
+    joined,
+    ranks,
+    starts,
     tops,
-    staged,
+    down,
+    onward,
     turned,
     x_sem,
     in_sem,
     out_sem,
     g_sem,
     table_sem,
-    z_send,
-    z_recv,
+    up_send,
+    up_recv,
+    join_send,
+    join_recv,
     y_send,
     y_recv,
-    e_send,
-    e_recv,
+    down_send,
+    down_recv,
     fz_send,
     fz_recv,
-    fl_send,
-    fl_recv,
     fy_send,
     fy_recv,
     fc_send,
@@ -186,9 +189,9 @@
     zl, core = d // 2, d % 2
     away = t != d
 
-    def x_load(pair):
-        at = pair_lanes(pair)
-        return pltpu.make_async_copy(x_hbm.at[:, at], xv.at[:, at], x_sem.at[pair])
+    def x_load(n):
+        at = pl.ds(pl.multiple_of(n * 4 * P_SIZE, 4 * P_SIZE), 4 * P_SIZE)
+        return pltpu.make_async_copy(x_hbm.at[:, at], xv.at[:, at], x_sem.at[n])
 
     loads = [
         pltpu.make_async_copy(src, dst, in_sem.at[n])
@@ -218,9 +221,9 @@
 
     loads[0].start()
     loads[1].start()
-    for c in range(CH):
+    for half in range(2):
         for q in range(nz):
-            x_load(CH * q + c).start()
+            x_load(2 * q + half).start()
     for load in loads[2:]:
         load.start()
     spread_ref[...] = spread_matrix(spread_ref.shape)
@@ -231,24 +234,31 @@
     def y_dev(i):
         return (((y + i) % ny) * nz + z, t, d)
 
-    def cross_dev(i):
-        return (y * nz + (z + i) % nz, d, t)
-
-    zl_dev = (s, t, (1 - zl) * 2 + core)
+    def cross_dev(i, l):
+        return (y * nz + (z + i) % nz, d, (zl + l) % 2 * 2 + t % 2)
+
     core_dev = (s, t, zl * 2 + 1 - core)
 
+    def own_source(i, p):
+        return jnp.logical_and(d == t, p == t // 2) if i == 0 else False
+
     barrier = pltpu.get_barrier_semaphore()
-    others = [z_dev(i) for i in range(1, nz)] + [y_dev(i) for i in range(1, ny)]
-    others += [zl_dev, core_dev]
+    others = [z_dev(1), z_dev(nz - 1)] + [y_dev(i) for i in range(1, ny)] + [core_dev]
     for dev in others:
         pl.semaphore_signal(barrier, inc=1, device_id=dev, device_id_type=MESH)
-
-    @pl.when(away)
-    def _():
-        for i in range(nz):
-            pl.semaphore_signal(barrier, inc=1, device_id=cross_dev(i), device_id_type=MESH)
-
-    pl.semaphore_wait(barrier, jnp.where(away, len(others) + nz, len(others)))
+    for i in range(nz):
+        for p in range(2):
+            prompt = 2 * p + core
+
+            @pl.when(jnp.logical_not(own_source(i, p)))
+            def _():
+                pl.semaphore_signal(
+                    barrier, inc=1, device_id=(y * nz + (z + i) % nz, prompt, t),
+                    device_id_type=MESH,
+                )
+
+    count = len(others) + 2 * nz
+    pl.semaphore_wait(barrier, jnp.where(away, count, count - 1))
 
     def copy(src, dst, send, recv, dev):
         return pltpu.make_async_remote_copy(
@@ -256,37 +266,69 @@
             device_id_type=MESH,
         )
 
-    def z_copy(c, i):
+    def turn(q, c):
+        return (0, 1, 1 - c % 2, 0)[q]
+
+    def place(q, c):
+        j = (z + nz - q) % nz
+        return j + turn(q, c) * (3 - 2 * j)
+
+    def near(q, c, step):
+        return z_dev(nz + step * (1 - 2 * turn(q, c)))
+
+    def order(q, c):
+        f = turn(q, c)
+        return ((1, 0, 2), (2, 0, 1), (2 - 2 * f, 1, 2 * f), (0, 2, 1))[q]
+
+    def end_copy(q, c):
         return copy(
-            s_ref.at[CH * ((z + i) % nz) + c], got.at[z, c], z_send.at[c, i - 1],
-            z_recv.at[c, i - 1], z_dev(i),
-        )
-
-    def y_copy(c, i):
+            s_ref.at[CH * q + c], ranks.at[q, c, order(q, c)[1]], up_send.at[q, c],
+            up_recv.at[q, c], near(q, c, 1),
+        )
+
+    def far_copy(q, c):
         return copy(
-            tops.at[y, c], tops.at[y, c], y_send.at[c, i - 1], y_recv.at[c, i - 1], y_dev(i)
-        )
-
-    def e_copy(c, i):
+            s_ref.at[CH * q + c], first.at[q, c], up_send.at[q, c], up_recv.at[q, c],
+            near(q, c, -1),
+        )
+
+    def join_copy(q, c):
         return copy(
-            staged.at[(z + i) % nz, c], e_ref.at[CH * z + c], e_send.at[c, i - 1],
-            e_recv.at[c, i - 1], z_dev(i),
-        )
-
-    def fz_copy(c, i):
+            joined.at[q, c], ranks.at[q, c, order(q, c)[2]], join_send.at[q, c],
+            join_recv.at[q, c], near(q, c, -1),
+        )
+
+    def y_copy(q, c, i):
         return copy(
-            turned.at[c, pl.ds(32 * y, 32)], g_ref.at[c, y, t % 2, t // 2, z], fz_send.at[c, i],
-            fz_recv.at[c, i], cross_dev(i),
-        )
-
-    def fl_copy(c):
-        ref = g_ref.at[c, y, core, zl]
-        return copy(ref, ref, fl_send.at[c], fl_recv.at[c], zl_dev)
-
-    def fy_copy(c, i, other):
-        ref = g_ref.at[c, y, core, 1 - zl if other else zl]
-        n = 3 * other + i - 1
-        return copy(ref, ref, fy_send.at[c, n], fy_recv.at[c, n], y_dev(i))
+            tops.at[q, c, y], tops.at[q, c, y], y_send.at[q, c, i - 1], y_recv.at[q, c, i - 1],
+            y_dev(i),
+        )
+
+    def down_copy(q, c, n):
+        return copy(
+            starts.at[q, c, order(q, c)[1 + n]], down.at[q, c], down_send.at[q, c, n],
+            down_recv.at[q, c], near(q, c, 2 * n - 1),
+        )
+
+    def onward_copy(q, c):
+        return copy(
+            onward.at[q, c], down.at[q, c], down_send.at[q, c, 0], down_recv.at[q, c],
+            near(q, c, 1),
+        )
+
+    def fz_copy(q, c, i, l):
+        return copy(
+            turned.at[q, c, pl.ds(32 * y, 32)], g_ref.at[c, y, t % 2, t // 2, q],
+            fz_send.at[q, c, i + nz * l], fz_recv.at[q, c, t // 2], cross_dev(i, l),
+        )
+
+    def fz_wait(q, c, p):
+        ref = g_ref.at[c, y, core, p, q]
+        copy(ref, ref, fz_send.at[q, c, 0], fz_recv.at[q, c, p], core_dev).wait_recv()
+
+    def fy_copy(c, i):
+        ref = g_ref.at[c, y, core]
+        return copy(ref, ref, fy_send.at[c, i - 1], fy_recv.at[c, i - 1], y_dev(i))
 
     def fc_copy(c, i):
         ref = g_ref.at[c, (y + ny - i) % ny, core]
@@ -295,21 +337,28 @@
     loads[0].wait()
     row = lax.broadcasted_iota(jnp.int32, (B, B), 0)
     col = lax.broadcasted_iota(jnp.int32, (B, B), 1)
-    upper = (row <= col).astype(F32)
+    upper = (row <= col).astype(F32).astype(BF16)
     lead = jnp.zeros((1, 2 * heads), F32)
     leads = []
+    rows_of = []
+    for k in range(blocks):
+        dec = dv[:, k * B : (k + 1) * B] * LOG2E
+        hi = dec.astype(BF16)
+        mid = (dec - hi.astype(F32)).astype(BF16)
+        low = (dec - hi.astype(F32) - mid.astype(F32)).astype(BF16)
+        three = jnp.concatenate([hi, mid, low], axis=1)
+        rows_of += [three, three]
+    sums = dot(jnp.concatenate(rows_of, axis=0), jnp.concatenate([upper] * 3, axis=0))
     for k in range(blocks):
         at = pl.ds(k * B, B)
-        dec = dv[:, at]
-        sums = dot(jnp.concatenate([dec, dec], axis=0) * LOG2E, upper, precision=HIGH)
-        cum[:, at] = sums
-        cum_t[at, :] = sums.T
+        mine = sums[k * 2 * heads : (k + 1) * 2 * heads]
+        cum[:, at] = mine
+        cum_t[at, :] = mine.T
         leads.append(lead)
         lead = lead + cum_t[k * B + B - 1 : k * B + B, :]
     for k in range(blocks):
         at = pl.ds(k * B, B)
         whole = cum_t[at, :] + leads[k]
-        grown[at, :] = hi_low(jnp.exp2(whole))
         remain[at, :] = hi_low(jnp.exp2(jnp.minimum(lead - whole, 0.0)))
     keep = hi_low(jnp.broadcast_to(jnp.exp2(lead), (16, 2 * heads)))
 
@@ -319,33 +368,42 @@
             at = pl.ds(k * B, B)
             bt[g, :, at] = bv[at, g * N : (g + 1) * N].T
 
-    def own_state(c, carry):
+    def at_place(q, c, where, act):
+        @pl.when(place(q, c) == where)
+        def _():
+            act()
+
+    def own_state(half, carry):
         left = remain[...]
         for q in range(nz):
-            pair = CH * q + c
             g = q * CH * 2 // per
-            x_load(pair).wait()
-            at = pair_lanes(pair)
+            x_load(2 * q + half).wait()
+            at = pl.ds(pl.multiple_of((2 * q + half) * 4 * P_SIZE, 4 * P_SIZE), 4 * P_SIZE)
             sp = spread_ref[:, at]
             scaled = (xv[:, at].astype(F32) * dot(left, sp)).astype(BF16)
-            s_ref[pair, 0:N] = dot(bt[g], scaled)
-            s_ref[pair, N : N + 8] = dot(keep, sp)[0:8]
-        for i in range(1, nz):
-            z_copy(c, i).start()
-        got[z, c] = s_ref[CH * z + c]
+            both = dot(bt[g], scaled)
+            fades = dot(keep, sp)
+            for n in range(2):
+                c = 2 * half + n
+                pair = CH * q + c
+                here = slice(n * 2 * P_SIZE, (n + 1) * 2 * P_SIZE)
+                s_ref[pair, 0:N] = both[:, here]
+                s_ref[pair, N : N + 8] = fades[0:8, here]
+                at_place(q, c, 0, lambda: end_copy(q, c).start())
+                at_place(q, c, 3, lambda: far_copy(q, c).start())
+
+                @pl.when(place(q, c) == 1)
+                def _():
+                    ranks[q, c, order(q, c)[0]] = s_ref[pair]
+
         return carry
 
-    with jax.named_scope("own_state"):
-        lax.fori_loop(0, CH, own_state, 0)
+    lax.fori_loop(0, 2, own_state, 0)
     for load in loads[2:]:
         load.wait()
-    with jax.named_scope("decode_tables"):
-        decode_tables(
-            sx_ref, sb_ref, sc_ref, sd_ref, spread_ref, pre_ref, reach_ref, push_ref, last_ref,
-            cc_ref, bb_ref,
-        )
-    for table in tables:
-        table.start()
+    for k in range(blocks):
+        at = pl.ds(k * B, B)
+        grown[at, :] = hi_low(jnp.exp2(cum_t[at, :] + leads[k]))
     state[...] = jnp.zeros((N, wide), F32)
     lane = lax.broadcasted_iota(jnp.int32, (B, 2 * P_SIZE), 1)
 
@@ -384,71 +442,105 @@
                 inner = dot(jnp.concatenate(weights, axis=1), both)
                 part[rows, pl.ds((g * per + 2 * n) * P_SIZE, 2 * P_SIZE)] = inner + carried[:, here]
 
-    def stage_a(c):
-        for i in range(1, nz):
-            z_copy(c, i).wait_recv()
-        top = got[0, c, 0:N]
-        kept = got[0, c, N : N + 8]
-        for k in range(1, nz):
-            a = got[k, c, N : N + 8]
-            top = top * a[0:1] + got[k, c, 0:N]
+    def join(q, c):
+        far_copy(q, c).wait_recv()
+        pair = CH * q + c
+        f = turn(q, c) == 1
+        own, other = s_ref[pair, 0:N], first[q, c, 0:N]
+        keep, fade = s_ref[pair, N : N + 8], first[q, c, N : N + 8]
+        joined[q, c, 0:N] = jnp.where(f, other, own) * jnp.where(f, keep[0:1], fade[0:1]) + (
+            jnp.where(f, own, other)
+        )
+        joined[q, c, N : N + 8] = keep * fade
+        join_copy(q, c).start()
+
+    def gather(q, c):
+        end_copy(q, c).wait_recv()
+        join_copy(q, c).wait_recv()
+        top = ranks[q, c, 0, 0:N]
+        kept = ranks[q, c, 0, N : N + 8]
+        for k in range(1, 3):
+            a = ranks[q, c, k, N : N + 8]
+            top = top * a[0:1] + ranks[q, c, k, 0:N]
             kept = kept * a
-        tops[y, c, 0:N] = top
-        tops[y, c, N : N + 8] = kept
+        tops[q, c, y, 0:N] = top
+        tops[q, c, y, N : N + 8] = kept
         for i in range(1, ny):
-            y_copy(c, i).start()
-
-    def stage_b(c):
+            y_copy(q, c, i).start()
+
+    def spread_out(q, c):
         for i in range(1, ny):
-            y_copy(c, i).wait_recv()
+            y_copy(q, c, i).wait_recv()
         enter = jnp.zeros((N, 2 * P_SIZE), F32)
         last = enter
         for k in range(ny):
-            a = tops[k, c, N : N + 1]
-            top = tops[k, c, 0:N]
+            a = tops[q, c, k, N : N + 1]
+            top = tops[q, c, k, 0:N]
             enter = jnp.where(k < y, enter * a + top, enter)
             last = last * a + top
-        turned[c] = last.T
+        turned[q, c] = last.T
+        for k in range(3):
+            starts[q, c, k] = enter
+            if k < 2:
+                enter = enter * ranks[q, c, k, N : N + 1] + ranks[q, c, k, 0:N]
+        for l in range(2):
+            for i in range(nz):
+                if i or l:
+                    fz_copy(q, c, i, l).start()
 
         @pl.when(away)
         def _():
-            fz_copy(c, 0).start()
+            fz_copy(q, c, 0, 0).start()
 
         @pl.when(jnp.logical_not(away))
         def _():
-            g_ref[c, y, core, zl, z] = turned[c, pl.ds(32 * y, 32)]
-
-        for i in range(1, nz):
-            fz_copy(c, i).start()
-        for k in range(nz):
-            staged[k, c] = enter
-            if k < nz - 1:
-                enter = enter * got[k, c, N : N + 1] + got[k, c, 0:N]
-        e_ref[CH * z + c] = staged[z, c]
-        for i in range(1, nz):
-            e_copy(c, i).start()
-
-    def stage_c(c):
-        @pl.when(away)
+            g_ref[c, y, core, zl, q] = turned[q, c, pl.ds(32 * y, 32)]
+
+        for n in (1, 0):
+            down_copy(q, c, n).start()
+        e_ref[CH * q + c] = starts[q, c, order(q, c)[0]]
+
+    def pass_on(q, c):
+        down_copy(q, c, 1).wait_recv()
+        pair = CH * q + c
+        f = turn(q, c) == 1
+        came = down[q, c]
+        own, other = s_ref[pair, 0:N], first[q, c, 0:N]
+        a = jnp.where(f, first[q, c, N : N + 1], s_ref[pair, N : N + 1])
+        after = came * a + jnp.where(f, other, own)
+        onward[q, c] = jnp.where(f, came, after)
+        onward_copy(q, c).start()
+        e_ref[pair] = jnp.where(f, after, came)
+
+    def arrive(q, c):
+        @pl.when(place(q, c) % 3 == 0)
         def _():
-            fz_copy(c, 0).wait_recv()
-
-        for i in range(1, nz):
-            fz_copy(c, i).wait_recv()
-        fl_copy(c).start()
+            onward_copy(q, c).wait_recv()
+            e_ref[CH * q + c] = down[q, c]
+
+    def each(act, where):
+        def stage(c):
+            for q in range(nz):
+                at_place(q, c, where, functools.partial(act, q, c))
+
+        return stage
+
+    def stage_e(c):
+        for q in range(nz):
+            for p in range(2):
+                mine = jnp.logical_and(place(q, c) == 1, jnp.logical_and(d == t, p == t // 2))
+
+                @pl.when(jnp.logical_not(mine))
+                def _():
+                    fz_wait(q, c, p)
+
         for i in range(1, ny):
-            fy_copy(c, i, 0).start()
+            fy_copy(c, i).start()
+        fc_copy(c, 0).start()
 
     def stage_d(c):
-        fl_copy(c).wait_recv()
         for i in range(1, ny):
-            fy_copy(c, i, 1).start()
-        fc_copy(c, 0).start()
-
-    def stage_e(c):
-        for i in range(1, ny):
-            fy_copy(c, i, 0).wait_recv()
-            fy_copy(c, i, 1).wait_recv()
+            fy_copy(c, i).wait_recv()
             fc_copy(c, i).start()
 
     def stage_f(c):
@@ -457,8 +549,8 @@
         g_store(c).start()
 
     def close(c):
-        for i in range(1, nz):
-            e_copy(c, i).wait_recv()
+        for q in range(nz):
+            arrive(q, c)
         for q in range(nz):
             pair = CH * q + c
             g = q * CH * 2 // per
@@ -469,59 +561,77 @@
             y_store(pair).start()
 
     stages = (
-        (stage_a, 0), (stage_b, 1), (stage_c, 2), (stage_d, 3), (stage_e, 4), (stage_f, 5),
-        (close, CLOSE),
+        (each(join, 2), 0), (each(gather, 1), 1), (each(spread_out, 1), 2), (stage_e, 4),
+        (each(pass_on, 2), 4), (stage_d, 6), (stage_f, 7),
     )
-    for k in range(EARLY):
-        block(k)
-
     def step(n, carry):
         for stage, after in stages:
 
             @pl.when(jnp.logical_and(n >= after, n < after + CH))
             def _():
-                with jax.named_scope(stage.__name__):
-                    stage(n - after)
-
-        @pl.when(n < blocks - EARLY)
+                stage(n - after)
+
+        @pl.when(n < blocks)
         def _():
-            with jax.named_scope("block"):
-                block(n + EARLY)
+            block(n)
+
+        @pl.when(n == TABLES)
+        def _():
+            decode_tables(
+                sx_ref, sb_ref, sc_ref, sd_ref, spread_ref, pre_ref, reach_ref, push_ref,
+                last_ref, cc_ref, bb_ref,
+            )
+            for table in tables:
+                table.start()
+
+        @pl.when(n >= CLOSE)
+        def _():
+            close(n - CLOSE)
 
         return carry
 
     lax.fori_loop(0, CLOSE + CH, step, 0)
 
     def drain(c, carry):
-        for i in range(1, nz):
-            z_copy(c, i).wait_send()
-            e_copy(c, i).wait_send()
-            fz_copy(c, i).wait_send()
+        for q in range(nz):
+            at_place(q, c, 0, lambda: end_copy(q, c).wait_send())
+            at_place(q, c, 3, lambda: far_copy(q, c).wait_send())
+
+            @pl.when(place(q, c) == 1)
+            def _():
+                for n in range(2):
+                    down_copy(q, c, n).wait_send()
+                for i in range(1, ny):
+                    y_copy(q, c, i).wait_send()
+                for l in range(2):
+                    for i in range(nz):
+                        if i or l:
+                            fz_copy(q, c, i, l).wait_send()
+
+                @pl.when(away)
+                def _():
+                    fz_copy(q, c, 0, 0).wait_send()
+
+            @pl.when(place(q, c) == 2)
+            def _():
+                join_copy(q, c).wait_send()
+                onward_copy(q, c).wait_send()
+
+            y_store(CH * q + c).wait()
         for i in range(1, ny):
-            y_copy(c, i).wait_send()
-            fy_copy(c, i, 0).wait_send()
-            fy_copy(c, i, 1).wait_send()
+            fy_copy(c, i).wait_send()
         for i in range(ny):
             fc_copy(c, i).wait_send()
         g_store(c).wait()
-        for q in range(nz):
-            y_store(CH * q + c).wait()
-        fl_copy(c).wait_send()
-
-        @pl.when(away)
-        def _():
-            fz_copy(c, 0).wait_send()
-
         return carry
 
-    with jax.named_scope("drain"):
-        lax.fori_loop(0, CH, drain, 0)
-        for table in tables:
-            table.wait()
-
-
-CLOSE = 6
-EARLY = 2
+    lax.fori_loop(0, CH, drain, 0)
+    for table in tables:
+        table.wait()
+
+
+CLOSE = 7
+TABLES = 8
 
 
 def core(x, b, c, decay, sx, sb, sc, sd, nz, ny):
@@ -570,20 +680,24 @@
             pltpu.VMEM((pairs, N + 8, 2 * P_SIZE), F32),
             pltpu.VMEM((pairs,) + pair_shape, F32),
             pltpu.VMEM((nz, CH, N + 8, 2 * P_SIZE), F32),
-            pltpu.VMEM((ny, CH, N + 8, 2 * P_SIZE), F32),
+            pltpu.VMEM((nz, CH, N + 8, 2 * P_SIZE), F32),
+            pltpu.VMEM((nz, CH, 3, N + 8, 2 * P_SIZE), F32),
+            pltpu.VMEM((nz, CH, 3) + pair_shape, F32),
+            pltpu.VMEM((nz, CH, ny, N + 8, 2 * P_SIZE), F32),
             pltpu.VMEM((nz, CH) + pair_shape, F32),
-            pltpu.VMEM((CH, 2 * P_SIZE, N), F32),
-            dma((pairs,)),
+            pltpu.VMEM((nz, CH) + pair_shape, F32),
+            pltpu.VMEM((nz, CH, 2 * P_SIZE, N), F32),
+            dma((2 * nz,)),
             dma((7,)),
             dma((pairs,)),
             dma((CH,)),
             dma((6,)),
+            dma((nz, CH)), dma((nz, CH)),
+            dma((nz, CH)), dma((nz, CH)),
+            dma((nz, CH, 3)), dma((nz, CH, 3)),
+            dma((nz, CH, 2)), dma((nz, CH)),
+            dma((nz, CH, 8)), dma((nz, CH, 2)),
             dma((CH, 3)), dma((CH, 3)),
-            dma((CH, 3)), dma((CH, 3)),
-            dma((CH, 3)), dma((CH, 3)),
-            dma((CH, 4)), dma((CH, 4)),
-            dma((CH,)), dma((CH,)),
-            dma((CH, 6)), dma((CH, 6)),
             dma((CH, 4)), dma((CH, 4)),
         ],
         compiler_params=pltpu.CompilerParams(
@@ -594,39 +708,91 @@
 
 
 def decode_kernel(
-    row_ref, slot_ref, y_in, g_ref, pre_ref, reach_ref, push_ref, last_ref, cc_ref, bb_ref,
-    y_out, out_ref, cache_ref,
+    row_ref, slot_ref, y_hbm, g_hbm, *rest
 ):
-    chunk = pl.program_id(0)
+    tables_hbm, rest = rest[:6], rest[6:]
+    y_out, out_hbm, cache_hbm, y_ref, g_ref = rest[:5]
+    tables, rest = rest[5:11], rest[11:]
+    pre_ref, reach_ref, push_ref, last_ref, cc_ref, bb_ref = tables
+    out_ref, cache_ref, load_sem, y_load_sem, y_sem, g_sem, out_sem, cache_sem = rest
     rows = pre_ref.shape[0]
-    y_out[...] = y_in[...]
-
-    for zi in range(4):
-        g = zi // 2
-        pair = CH * zi + chunk
-        at = pair_lanes(pair)
-        seen = []
-        for prompt in range(4):
-            f = g_ref[0, :, prompt % 2, prompt // 2, zi].reshape(2 * P_SIZE, N)
-            hi = f.astype(BF16)
-            low = (f - hi.astype(F32)).astype(BF16)
-            seen.append(dot(cc_ref[g], jnp.concatenate([hi, low], axis=1), ((1,), (1,))))
-        gain = dot(push_ref[at, :], bb_ref[g])
-        for r in range(rows):
-            mine = row_ref[r]
-            pick = seen[0][r * STEPS : (r + 1) * STEPS]
-            for prompt in range(1, 4):
-                pick = jnp.where(mine == prompt, seen[prompt][r * STEPS : (r + 1) * STEPS], pick)
-            out_ref[:, r, at] = (pick * reach_ref[r, :, at] + pre_ref[r, :, at]).astype(BF16)
-            f = g_ref[0, :, mine % 2, mine // 2, zi].reshape(2 * P_SIZE, N)
-            kept = jnp.concatenate(
-                [
-                    jnp.broadcast_to(last_ref[r, pl.ds(2 * pair + n, 1), :], (P_SIZE, N))
-                    for n in range(2)
-                ],
-                axis=0,
-            )
-            cache_ref[slot_ref[r], zi, 0] = (f * kept + gain[:, r * N : (r + 1) * N]).astype(BF16)
+    loads = [
+        pltpu.make_async_copy(src, dst, load_sem.at[n])
+        for n, (src, dst) in enumerate(zip(tables_hbm, tables))
+    ]
+
+    def g_load(chunk):
+        return pltpu.make_async_copy(g_hbm.at[chunk], g_ref.at[chunk], g_sem.at[chunk])
+
+    height = y_ref.shape[0] // CH
+
+    def y_load(n):
+        at = pl.ds(pl.multiple_of(n * height, height), height)
+        return pltpu.make_async_copy(y_hbm.at[at], y_ref.at[at], y_load_sem.at[n])
+
+    def y_store(n):
+        at = pl.ds(pl.multiple_of(n * height, height), height)
+        return pltpu.make_async_copy(y_ref.at[at], y_out.at[at], y_sem.at[n])
+
+    for load in loads:
+        load.start()
+    g_load(0).start()
+    g_load(1).start()
+    for n in range(CH):
+        y_load(n).start()
+    for n in range(2, CH):
+        g_load(n).start()
+    for load in loads:
+        load.wait()
+
+    def cache_store(chunk):
+        return pltpu.make_async_copy(
+            cache_ref.at[chunk], cache_hbm.at[:, :, chunk], cache_sem.at[chunk]
+        )
+
+    def work(chunk, carry):
+        g_load(chunk).wait()
+        for zi in range(4):
+            g = zi // 2
+            pair = CH * zi + chunk
+            at = pair_lanes(pair)
+            seen = []
+            for prompt in range(4):
+                f = g_ref[chunk, :, prompt % 2, prompt // 2, zi].reshape(2 * P_SIZE, N)
+                hi = f.astype(BF16)
+                low = (f - hi.astype(F32)).astype(BF16)
+                seen.append(dot(cc_ref[g], jnp.concatenate([hi, low], axis=1), ((1,), (1,))))
+            gain = dot(push_ref[at, :], bb_ref[g])
+            for r in range(rows):
+                mine = row_ref[r]
+                part = slice(r * STEPS, (r + 1) * STEPS)
+                pick = seen[0][part]
+                for prompt in range(1, 4):
+                    pick = jnp.where(mine == prompt, seen[prompt][part], pick)
+                out_ref[:, r, at] = (pick * reach_ref[r, :, at] + pre_ref[r, :, at]).astype(BF16)
+                f = g_ref[chunk, :, mine % 2, mine // 2, zi].reshape(2 * P_SIZE, N)
+                kept = jnp.concatenate(
+                    [
+                        jnp.broadcast_to(last_ref[r, pl.ds(2 * pair + n, 1), :], (P_SIZE, N))
+                        for n in range(2)
+                    ],
+                    axis=0,
+                )
+                cache_ref[chunk, slot_ref[r], zi] = (
+                    f * kept + gain[:, r * N : (r + 1) * N]
+                ).astype(BF16)
+        cache_store(chunk).start()
+        y_load(chunk).wait()
+        y_store(chunk).start()
+        return carry
+
+    lax.fori_loop(0, CH, work, 0)
+    out_store = pltpu.make_async_copy(out_ref, out_hbm, out_sem)
+    out_store.start()
+    for chunk in range(CH):
+        y_store(chunk).wait()
+        cache_store(chunk).wait()
+    out_store.wait()
 
 
 def decode(row_prompt, cache_slot, y, g, tables, shape):
@@ -634,34 +800,29 @@
     nz = g.shape[4]
     heads = shape[2] // P_SIZE
     smem = pl.BlockSpec(memory_space=pltpu.SMEM)
-    part = pl.BlockSpec((y.shape[0] // CH, y.shape[1]), lambda i: (i, 0))
-
-    def whole(s):
-        return pl.BlockSpec(s, lambda i: (0,) * len(s))
-
+    hbm = pl.BlockSpec(memory_space=pl.ANY)
+    dma = pltpu.SemaphoreType.DMA
     seq, out, cache = pl.pallas_call(
         decode_kernel,
-        grid=(CH,),
         out_shape=(
             jax.ShapeDtypeStruct(y.shape, BF16),
             jax.ShapeDtypeStruct(shape, BF16),
             jax.ShapeDtypeStruct((rows, nz, CH, 2 * P_SIZE, N), BF16),
         ),
-        in_specs=[
-            smem,
-            smem,
-            part,
-            pl.BlockSpec((1,) + g.shape[1:], lambda i: (i, 0, 0, 0, 0, 0, 0)),
-        ]
-        + [whole(a.shape) for a in tables],
-        out_specs=(
-            part,
-            whole(shape),
-            pl.BlockSpec((rows, nz, 1, 2 * P_SIZE, N), lambda i: (0, 0, i, 0, 0)),
-        ),
-        compiler_params=pltpu.CompilerParams(
-            dimension_semantics=("arbitrary",), vmem_limit_bytes=60 * MIB
-        ),
+        in_specs=[smem, smem] + [hbm] * (2 + len(tables)),
+        out_specs=(hbm, hbm, hbm),
+        scratch_shapes=[pltpu.VMEM(a.shape, a.dtype) for a in (y, g, *tables)]
+        + [
+            pltpu.VMEM(shape, BF16),
+            pltpu.VMEM((CH, rows, nz, 2 * P_SIZE, N), BF16),
+            dma((len(tables),)),
+            dma((CH,)),
+            dma((CH,)),
+            dma((CH,)),
+            dma(()),
+            dma((CH,)),
+        ],
+        compiler_params=pltpu.CompilerParams(vmem_limit_bytes=60 * MIB),
         name="decode",
     )(row_prompt, cache_slot, y, g, *tables)
     return seq, out, cache.reshape(rows, heads, P_SIZE, N)

time: 101 us -> 97.3 us (0.963); the launches traced: 99.5 us -> 97.2 us
  Pallas kernels: 98.9 us -> 96.6 us
    pallas_call x1, Pallas kernels: 91.1 us -> 89.1 us  [core(): pl.pallas_call(functools.partial(core_kernel, (nz, ny)), out_shape=outs,...]
where the time goes in v3:
time: 97.3 us; the launch traced here: 97.2 us
  Pallas kernels  96.6 us (99%)
    pallas_call x1, Pallas kernels, core(): pl.pallas_call(functools.partial(core_kernel, (nz, ny)), out_shape=outs,...  89.1 us
    pallas_call x1, Pallas kernels, decode(): pl.pallas_call(decode_kernel, out_shape=(jax.ShapeDtypeStruct(y.shape, BF...  7.54 us

profile of v3, /device:TPU:7, one launch (start us, length us, event | category | flops | bytes accessed | tf_op | source)
XLA Modules:
  0.0 97.2 jit_solution(11863016251209144857)
XLA Ops:
  0.6 89.1 %core.1 = (bf16[1024,2048]{1,0:T(8,128)(2,1)}, f32[4,4,2,2,4,32,128]{6,5,4,3,2,1,0:T(8,128)}, f32[4,8,2048]{2,1,0:T(8,128)}, f32[4,8,2048]{2,1,0:T(8,128)}, bf16...) custom-call(bf16[1024,2048]{1,0:T(8,128)(2,1)} %bitcast.6, ...), custom_call_target="tpu_custom_call" | custom-call | tf_op jit(solution)/shard_map/core/pallas_call | solution.py:655
  89.7 7.5 %decode.1 = (bf16[1024,2048]{1,0:T(8,128)(2,1)}, bf16[8,4,2048]{2,1,0:T(4,128)(2,1)}, bf16[4,4,4,128,128]{4,3,2,1,0:T(8,128)(2,1)}) custom-call(s32[4]{0:T(128)} %row_ref.1, s32[4]{0:T(128)} %slot_ref.1, bf16[1024,2048]{1,0:T(8,128)(2,1)} %get-tuple-element.14.y_hbm, f32[4,4,2,2,4,32,128]{6,5,4,3,2,1,0:T(8,128)} %get-tuple-element.15.g_hbm, ...), custom_call_target="tpu_custom_call" | custom-call | tf_op jit(solution)/shard_map/decode/pallas_call | solution.py:805

commit v4 on v3

--- a/solution.py
+++ b/solution.py
@@ -257,8 +257,6 @@
                     device_id_type=MESH,
                 )
 
-    count = len(others) + 2 * nz
-    pl.semaphore_wait(barrier, jnp.where(away, count, count - 1))
 
     def copy(src, dst, send, recv, dev):
         return pltpu.make_async_remote_copy(
@@ -398,6 +396,8 @@
 
         return carry
 
+    count = len(others) + 2 * nz
+    pl.semaphore_wait(barrier, jnp.where(away, count, count - 1))
     lax.fori_loop(0, 2, own_state, 0)
     for load in loads[2:]:
         load.wait()
@@ -496,9 +496,11 @@
         def _():
             g_ref[c, y, core, zl, q] = turned[q, c, pl.ds(32 * y, 32)]
 
+        e_ref[CH * q + c] = starts[q, c, order(q, c)[0]]
+
+    def send_down(q, c):
         for n in (1, 0):
             down_copy(q, c, n).start()
-        e_ref[CH * q + c] = starts[q, c, order(q, c)[0]]
 
     def pass_on(q, c):
         down_copy(q, c, 1).wait_recv()
@@ -561,8 +563,8 @@
             y_store(pair).start()
 
     stages = (
-        (each(join, 2), 0), (each(gather, 1), 1), (each(spread_out, 1), 2), (stage_e, 4),
-        (each(pass_on, 2), 4), (stage_d, 6), (stage_f, 7),
+        (each(join, 2), 0), (each(gather, 1), 1), (each(spread_out, 1), 2), (each(send_down, 1), 4),
+        (stage_e, 4), (each(pass_on, 2), 6), (stage_d, 6), (stage_f, 7),
     )
     def step(n, carry):
         for stage, after in stages:
@@ -630,7 +632,7 @@
         table.wait()
 
 
-CLOSE = 7
+CLOSE = 8
 TABLES = 8
 
 
@@ -751,6 +753,8 @@
         )
 
     def work(chunk, carry):
+        y_load(chunk).wait()
+        y_store(chunk).start()
         g_load(chunk).wait()
         for zi in range(4):
             g = zi // 2
@@ -782,8 +786,6 @@
                     f * kept + gain[:, r * N : (r + 1) * N]
                 ).astype(BF16)
         cache_store(chunk).start()
-        y_load(chunk).wait()
-        y_store(chunk).start()
         return carry
 
     lax.fori_loop(0, CH, work, 0)

time: 97.3 us -> 94 us (0.966)
  Pallas kernels: 96.6 us -> 93.2 us
    pallas_call x1, Pallas kernels: 89.1 us -> 86 us  [core(): pl.pallas_call(functools.partial(core_kernel, (nz, ny)), out_shape=outs,...]
where the time goes in v4:
time: 94 us; the launch traced here: 93.9 us
  Pallas kernels  93.2 us (99%)
    pallas_call x1, Pallas kernels, core(): pl.pallas_call(functools.partial(core_kernel, (nz, ny)), out_shape=outs,...  86 us
    pallas_call x1, Pallas kernels, decode(): pl.pallas_call(decode_kernel, out_shape=(jax.ShapeDtypeStruct(y.shape, BF...  7.22 us

profile of v4, /device:TPU:7, one launch (start us, length us, event | category | flops | bytes accessed | tf_op | source)
XLA Modules:
  0.0 93.9 jit_solution(17593439273472088340)
XLA Ops:
  0.6 86.0 %core.1 = (bf16[1024,2048]{1,0:T(8,128)(2,1)}, f32[4,4,2,2,4,32,128]{6,5,4,3,2,1,0:T(8,128)}, f32[4,8,2048]{2,1,0:T(8,128)}, f32[4,8,2048]{2,1,0:T(8,128)}, bf16...) custom-call(bf16[1024,2048]{1,0:T(8,128)(2,1)} %bitcast.6, ...), custom_call_target="tpu_custom_call" | custom-call | tf_op jit(solution)/shard_map/core/pallas_call | solution.py:657
  86.7 7.2 %decode.1 = (bf16[1024,2048]{1,0:T(8,128)(2,1)}, bf16[8,4,2048]{2,1,0:T(4,128)(2,1)}, bf16[4,4,4,128,128]{4,3,2,1,0:T(8,128)(2,1)}) custom-call(s32[4]{0:T(128)} %row_ref.1, s32[4]{0:T(128)} %slot_ref.1, bf16[1024,2048]{1,0:T(8,128)(2,1)} %get-tuple-element.14.y_hbm, f32[4,4,2,2,4,32,128]{6,5,4,3,2,1,0:T(8,128)} %get-tuple-element.15.g_hbm, ...), custom_call_target="tpu_custom_call" | custom-call | tf_op jit(solution)/shard_map/decode/pallas_call | solution.py:807

commit v5 on v4

--- a/solution.py
+++ b/solution.py
@@ -564,7 +564,7 @@
 
     stages = (
         (each(join, 2), 0), (each(gather, 1), 1), (each(spread_out, 1), 2), (each(send_down, 1), 4),
-        (stage_e, 4), (each(pass_on, 2), 6), (stage_d, 6), (stage_f, 7),
+        (stage_e, 4), (each(pass_on, 2), 5), (stage_d, 6), (stage_f, 7),
     )
     def step(n, carry):
         for stage, after in stages:

time: 94 us -> 94.9 us (level)
  no operation moved by 1% of the time
where the time goes in v5:
time: 94.9 us; the launch traced here: 93.9 us
  Pallas kernels  93.3 us (98%)
    pallas_call x1, Pallas kernels, core(): pl.pallas_call(functools.partial(core_kernel, (nz, ny)), out_shape=outs,...  86 us
    pallas_call x1, Pallas kernels, decode(): pl.pallas_call(decode_kernel, out_shape=(jax.ShapeDtypeStruct(y.shape, BF...  7.22 us

profile of v5, /device:TPU:7, one launch (start us, length us, event | category | flops | bytes accessed | tf_op | source)
XLA Modules:
  0.0 93.9 jit_solution(1112618949137824355)
XLA Ops:
  0.6 86.0 %core.1 = (bf16[1024,2048]{1,0:T(8,128)(2,1)}, f32[4,4,2,2,4,32,128]{6,5,4,3,2,1,0:T(8,128)}, f32[4,8,2048]{2,1,0:T(8,128)}, f32[4,8,2048]{2,1,0:T(8,128)}, bf16...) custom-call(bf16[1024,2048]{1,0:T(8,128)(2,1)} %bitcast.6, ...), custom_call_target="tpu_custom_call" | custom-call | tf_op jit(solution)/shard_map/core/pallas_call | solution.py:657
  86.7 7.2 %decode.1 = (bf16[1024,2048]{1,0:T(8,128)(2,1)}, bf16[8,4,2048]{2,1,0:T(4,128)(2,1)}, bf16[4,4,4,128,128]{4,3,2,1,0:T(8,128)(2,1)}) custom-call(s32[4]{0:T(128)} %row_ref.1, s32[4]{0:T(128)} %slot_ref.1, bf16[1024,2048]{1,0:T(8,128)(2,1)} %get-tuple-element.14.y_hbm, f32[4,4,2,2,4,32,128]{6,5,4,3,2,1,0:T(8,128)} %get-tuple-element.15.g_hbm, ...), custom_call_target="tpu_custom_call" | custom-call | tf_op jit(solution)/shard_map/decode/pallas_call | solution.py:807
